TPU v7x, 32 devices: a whole 2x2x4 slice. The times are simulated.
32 devices in a mesh: fsdp: 2 (over y), seq: 16 (over z, x, core).
Axes of the slice: x: 2, y: 2, z: 4, core: 2. Of those that a mesh axis runs over, the one named last changes fastest.
Arguments:
- tokens: bfloat16 [4, 1024, 1024], P('fsdp', 'seq'), may hold values from -6 to 6
- cotangent: bfloat16 [4, 1024, 1024], P('fsdp', 'seq'), may hold values from -6 to 6
- lengths: int32 [4], P('fsdp'), may hold values from 256 to 1024, as said below
- adapter_ids: int32 [4], P('fsdp'), may hold values from 0 to 7
- attn_weight: bfloat16 [1024, 4, 1024], P(('fsdp', 'seq')), may hold values from -2.25 to 2.25
- fc1_weight: bfloat16 [1024, 4096], P(('fsdp', 'seq')), may hold values from -0.1875 to 0.1875
- fc2_weight: bfloat16 [4096, 1024], P(('fsdp', 'seq')), may hold values from -0.09375 to 0.09375
- vectors: bfloat16 [1024, 8], P(('fsdp', 'seq')), may hold values from -0.6 to 1.4
- fc1_bias: bfloat16 [4096], P(('fsdp', 'seq')), may hold values from -1.1953125 to 1.1953125
- adapter_down: bfloat16 [1024, 8, 5, 16], P(('fsdp', 'seq')), may hold values from -0.1875 to 0.1875
- adapter_up: bfloat16 [1024, 8, 5, 16], P(('fsdp', 'seq')), may hold values from -0.75 to 0.75
- ff_adapters: bfloat16 [4096, 8, 2, 16], P(('fsdp', 'seq')), may hold values from -0.375 to 0.375
Outputs:
- layer_out: bfloat16 [4, 1024, 1024], P('fsdp', 'seq')
- input_grad: bfloat16 [4, 1024, 1024], P('fsdp', 'seq')
- down_grad: float32 [1024, 8, 5, 16], P(('fsdp', 'seq'))
- up_grad: float32 [1024, 8, 5, 16], P(('fsdp', 'seq'))
- ff_grad: float32 [4096, 8, 2, 16], P(('fsdp', 'seq'))
Inputs may be any that keep to these rules, and one draw needn't show every extreme that they name: `lengths`: in each aligned block of 2 slots one length is 1024.
All inputs are finite; a program needn't handle non-finite values.
Results may differ from a plain program's by a relative error of at most 0.019.
Values may be sent and summed in bfloat16 or wider, within the bound.
A program may use at most 320 MiB of HBM per device.

v0:
```python
from functools import partial
import math

import jax
import jax.numpy as jnp
from jax import lax
from jax.sharding import PartitionSpec as P

HEADS = 16
HEAD = 64
ADAPTERS = 8


NEG_FILL = -1e30
NORM_EPS = 1e-05


def split_heads(values_in):
    return values_in.reshape(values_in.shape[:-1] + (HEADS, HEAD))


def norm_rows(value, gain, shift):
    centered = value - jnp.mean(value, axis=-1, keepdims=True)
    scaled = centered * lax.rsqrt(jnp.mean(centered * centered, axis=-1, keepdims=True) + NORM_EPS)
    return scaled * gain + shift


def gelu_exact(value):
    return jax.nn.gelu(value, approximate=False)


def choose(onehot, table):
    return jnp.einsum("si,dikr->sdkr", onehot, table, preferred_element_type=jnp.float32).astype(
        jnp.bfloat16
    )


def unpack(gathered, onehot):
    attn_all, fc1_all, fc2_all, vector_all, bias_ff, down_all, up_all, ff_all = gathered
    return (
        attn_all,
        fc1_all,
        fc2_all,
        vector_all.astype(jnp.float32),
        bias_ff.astype(jnp.float32),
        choose(onehot, down_all),
        choose(onehot, up_all),
        choose(onehot, ff_all),
    )


def project(inputs, weight, down_table, up_table):
    frozen_part = jnp.einsum("spd,de->spe", inputs, weight, preferred_element_type=jnp.float32)
    inner_low = jnp.einsum(
        "spd,sdr->spr", inputs, down_table, preferred_element_type=jnp.float32
    ).astype(jnp.bfloat16)
    return (
        frozen_part
        + jnp.einsum("spr,ser->spe", inner_low, up_table, preferred_element_type=jnp.float32),
        inner_low,
    )


def project_back(inputs, inner_low, grad_out, weight, down_table, up_table):
    grad_inner = jnp.einsum(
        "spe,ser->spr", grad_out, up_table, preferred_element_type=jnp.float32
    ).astype(jnp.bfloat16)
    grad_in = jnp.einsum("spe,de->spd", grad_out, weight, preferred_element_type=jnp.float32)
    grad_in = grad_in + jnp.einsum(
        "spr,sdr->spd", grad_inner, down_table, preferred_element_type=jnp.float32
    )
    grad_up = jnp.einsum("spe,spr->ser", grad_out, inner_low, preferred_element_type=jnp.float32)
    grad_down = jnp.einsum("spd,spr->sdr", inputs, grad_inner, preferred_element_type=jnp.float32)
    return (grad_in, grad_down, grad_up)


def block_scores(query_heads, key_block, key_start, lengths):
    block_rows = key_block.shape[1]
    scores = jnp.einsum(
        "sqhd,skhd->shqk", query_heads, split_heads(key_block), preferred_element_type=jnp.float32
    )
    valid_keys = (key_start + jnp.arange(block_rows))[None, :] < lengths[:, None]
    return jnp.where(valid_keys[:, None, None, :], scores, NEG_FILL)


def score_grads(scores, logsum, row_delta, grad_heads, value_heads):
    probs = jnp.exp(scores - logsum[..., None])
    grad_probs = jnp.einsum(
        "sqhd,skhd->shqk", grad_heads, value_heads, preferred_element_type=jnp.float32
    )
    grad_scores = (probs * (grad_probs - row_delta[..., None])).astype(jnp.bfloat16)
    return (grad_scores, probs.astype(jnp.bfloat16))


def attend(query, all_keys, all_values, lengths):
    seq_span = all_keys.shape[1]
    block_rows = math.gcd(seq_span, 512)
    blocks = seq_span // block_rows
    query_heads = split_heads(query)
    slot_count, query_rows = (query.shape[0], query.shape[1])
    stats_shape = (slot_count, HEADS, query_rows)

    def stats_step(running, step_index):
        row_top, row_total = running
        offset = step_index * block_rows
        scores = block_scores(
            query_heads, lax.dynamic_slice_in_dim(all_keys, offset, block_rows, 1), offset, lengths
        )
        new_top = jnp.maximum(row_top, jnp.max(scores, axis=-1))
        row_total = row_total * jnp.exp(row_top - new_top) + jnp.sum(
            jnp.exp(scores - new_top[..., None]), axis=-1
        )
        return ((new_top, row_total), None)

    start_top = jnp.full(stats_shape, NEG_FILL, jnp.float32)
    (row_top, row_total), _ = lax.scan(
        stats_step, (start_top, jnp.zeros(stats_shape, jnp.float32)), jnp.arange(blocks)
    )
    logsum = row_top + jnp.log(row_total)

    def mix_step(running, step_index):
        offset = step_index * block_rows
        scores = block_scores(
            query_heads, lax.dynamic_slice_in_dim(all_keys, offset, block_rows, 1), offset, lengths
        )
        weights_low = jnp.exp(scores - logsum[..., None]).astype(jnp.bfloat16)
        value_heads = split_heads(lax.dynamic_slice_in_dim(all_values, offset, block_rows, 1))
        return (
            running
            + jnp.einsum(
                "shqk,skhd->sqhd", weights_low, value_heads, preferred_element_type=jnp.float32
            ),
            None,
        )

    mixed_heads, _ = lax.scan(
        mix_step, jnp.zeros(query_heads.shape, jnp.float32), jnp.arange(blocks)
    )
    return (mixed_heads.reshape(query.shape), logsum)


def query_side(query, all_keys, all_values, grad_low, logsum, row_delta, lengths):
    seq_span = all_keys.shape[1]
    block_rows = math.gcd(seq_span, 512)
    blocks = seq_span // block_rows
    query_heads = split_heads(query)
    grad_heads = split_heads(grad_low)
    slot_count = query.shape[0]
    width = query.shape[2]

    def step(running, step_index):
        offset = step_index * block_rows
        key_block = lax.dynamic_slice_in_dim(all_keys, offset, block_rows, 1)
        value_block = lax.dynamic_slice_in_dim(all_values, offset, block_rows, 1)
        scores = block_scores(query_heads, key_block, offset, lengths)
        grad_scores, weights_low = score_grads(
            scores, logsum, row_delta, grad_heads, split_heads(value_block)
        )
        grad_acc = running[0] + jnp.einsum(
            "shqk,skhd->sqhd",
            grad_scores,
            split_heads(key_block),
            preferred_element_type=jnp.float32,
        )
        key_part = jnp.einsum(
            "shqk,sqhd->skhd", grad_scores, query_heads, preferred_element_type=jnp.float32
        ).reshape(slot_count, block_rows, width)
        value_part = jnp.einsum(
            "shqk,sqhd->skhd", weights_low, grad_heads, preferred_element_type=jnp.float32
        ).reshape(slot_count, block_rows, width)
        key_buffer = lax.dynamic_update_slice_in_dim(running[1], key_part, offset, 1)
        value_buffer = lax.dynamic_update_slice_in_dim(running[2], value_part, offset, 1)
        return ((grad_acc, key_buffer, value_buffer), None)

    start = (jnp.zeros(query_heads.shape, jnp.float32),)
    empty = jnp.zeros((slot_count, seq_span, width), jnp.float32)
    start = start + (empty, empty)
    result, _ = lax.scan(step, start, jnp.arange(blocks))
    return (result[0].reshape(query.shape), result[1:])


def sum_by_adapter(picks, terms):
    return jnp.einsum("si,sdkr->dikr", picks, terms, precision=lax.Precision.HIGHEST)


def on_device(
    tokens,
    cotangent,
    lengths,
    adapter_ids,
    attn_weight,
    fc1_weight,
    fc2_weight,
    vectors,
    fc1_bias,
    adapter_down,
    adapter_up,
    ff_adapters,
):
    slot_count, slot_rows, width = tokens.shape
    row_start = lax.axis_index("seq") * slot_rows
    positions = row_start + jnp.arange(slot_rows)
    live_rows = (positions[None, :] < lengths[:, None]).astype(jnp.float32)[..., None]
    matches = adapter_ids[:, None] == jnp.arange(ADAPTERS)[None, :]
    onehot_low = matches.astype(jnp.bfloat16)
    onehot_full = matches.astype(jnp.float32)
    gathered = (
        lax.all_gather(attn_weight, ("fsdp", "seq"), axis=0, tiled=True),
        lax.all_gather(fc1_weight, ("fsdp", "seq"), axis=0, tiled=True),
        lax.all_gather(fc2_weight, ("fsdp", "seq"), axis=0, tiled=True),
        lax.all_gather(vectors, ("fsdp", "seq"), axis=0, tiled=True),
        lax.all_gather(fc1_bias, ("fsdp", "seq"), axis=0, tiled=True),
        lax.all_gather(adapter_down, ("fsdp", "seq"), axis=0, tiled=True),
        lax.all_gather(adapter_up, ("fsdp", "seq"), axis=0, tiled=True),
        lax.all_gather(ff_adapters, ("fsdp", "seq"), axis=0, tiled=True),
    )
    attn_all, fc1_all, fc2_all, vector_cols, bias_ff, down_pick, up_pick, ff_pick = unpack(
        gathered, onehot_low
    )
    query_pre, inner_query = project(
        tokens, attn_all[:, 0, :], down_pick[:, :, 0], up_pick[:, :, 0]
    )
    query = ((query_pre + vector_cols[:, 0]) * 0.125).astype(jnp.bfloat16)
    key_pre, inner_key = project(tokens, attn_all[:, 1, :], down_pick[:, :, 1], up_pick[:, :, 1])
    keys = key_pre.astype(jnp.bfloat16)
    value_pre, inner_value = project(
        tokens, attn_all[:, 2, :], down_pick[:, :, 2], up_pick[:, :, 2]
    )
    values = (value_pre + vector_cols[:, 1]).astype(jnp.bfloat16)
    all_keys, all_values = (
        lax.all_gather(keys, "seq", axis=1, tiled=True),
        lax.all_gather(values, "seq", axis=1, tiled=True),
    )
    attended, logsum = attend(query, all_keys, all_values, lengths)
    mixed = attended.astype(jnp.bfloat16)
    branch_pre, inner_branch = project(
        mixed, attn_all[:, 3, :], down_pick[:, :, 3], up_pick[:, :, 3]
    )
    first_sum = tokens.astype(jnp.float32) + branch_pre + vector_cols[:, 2]
    normed, first_back = jax.vjp(
        partial(norm_rows, gain=vector_cols[:, 4], shift=vector_cols[:, 5]), first_sum
    )
    normed_low = normed.astype(jnp.bfloat16)
    hidden_pre, inner_hidden = project(normed_low, fc1_all, down_pick[:, :, 4], ff_pick[:, :, 0])
    activated, gelu_back = jax.vjp(gelu_exact, hidden_pre + bias_ff)
    activated_low = activated.astype(jnp.bfloat16)
    out_pre, inner_out = project(activated_low, fc2_all, ff_pick[:, :, 1], up_pick[:, :, 4])
    second = normed + out_pre + vector_cols[:, 3]
    final, second_back = jax.vjp(
        partial(norm_rows, gain=vector_cols[:, 6], shift=vector_cols[:, 7]), second
    )
    layer_out = (final * live_rows).astype(jnp.bfloat16)
    regathered = (
        lax.all_gather(attn_weight, ("fsdp", "seq"), axis=0, tiled=True),
        lax.all_gather(fc1_weight, ("fsdp", "seq"), axis=0, tiled=True),
        lax.all_gather(fc2_weight, ("fsdp", "seq"), axis=0, tiled=True),
        lax.all_gather(vectors, ("fsdp", "seq"), axis=0, tiled=True),
        lax.all_gather(fc1_bias, ("fsdp", "seq"), axis=0, tiled=True),
        lax.all_gather(adapter_down, ("fsdp", "seq"), axis=0, tiled=True),
        lax.all_gather(adapter_up, ("fsdp", "seq"), axis=0, tiled=True),
        lax.all_gather(ff_adapters, ("fsdp", "seq"), axis=0, tiled=True),
    )
    attn_all, fc1_all, fc2_all, vector_cols, bias_ff, down_pick, up_pick, ff_pick = unpack(
        regathered, onehot_low
    )
    grad_final = cotangent.astype(jnp.float32) * live_rows
    (grad_second,) = second_back(grad_final)
    grad_out_low = grad_second.astype(jnp.bfloat16)
    grad_activated, down_of_fc2, up_of_fc2 = project_back(
        activated_low, inner_out, grad_out_low, fc2_all, ff_pick[:, :, 1], up_pick[:, :, 4]
    )
    (grad_hidden,) = gelu_back(grad_activated)
    grad_hidden_low = grad_hidden.astype(jnp.bfloat16)
    grad_normed, down_of_fc1, up_of_fc1 = project_back(
        normed_low, inner_hidden, grad_hidden_low, fc1_all, down_pick[:, :, 4], ff_pick[:, :, 0]
    )
    (grad_first,) = first_back(grad_normed + grad_second)
    grad_branch_low = grad_first.astype(jnp.bfloat16)
    grad_mixed, down_of_out, up_of_out = project_back(
        mixed,
        inner_branch,
        grad_branch_low,
        attn_all[:, 3, :],
        down_pick[:, :, 3],
        up_pick[:, :, 3],
    )
    grad_mixed_low = grad_mixed.astype(jnp.bfloat16)
    row_delta = jnp.einsum(
        "sqhd,sqhd->shq", split_heads(grad_mixed_low.astype(jnp.float32)), split_heads(attended)
    )
    grad_query, parts = query_side(
        query, all_keys, all_values, grad_mixed_low, logsum, row_delta, lengths
    )
    grad_keys, grad_values = (
        lax.psum_scatter(
            parts[0].astype(jnp.bfloat16), "seq", scatter_dimension=1, tiled=True
        ).astype(jnp.float32),
        lax.psum_scatter(
            parts[1].astype(jnp.bfloat16), "seq", scatter_dimension=1, tiled=True
        ).astype(jnp.float32),
    )
    grad_query_low = grad_query.astype(jnp.bfloat16) * 0.125
    grad_keys_low = grad_keys.astype(jnp.bfloat16)
    grad_values_low = grad_values.astype(jnp.bfloat16)
    grad_from_query, down_of_query, up_of_query = project_back(
        tokens, inner_query, grad_query_low, attn_all[:, 0, :], down_pick[:, :, 0], up_pick[:, :, 0]
    )
    grad_from_key, down_of_key, up_of_key = project_back(
        tokens, inner_key, grad_keys_low, attn_all[:, 1, :], down_pick[:, :, 1], up_pick[:, :, 1]
    )
    grad_from_value, down_of_value, up_of_value = project_back(
        tokens,
        inner_value,
        grad_values_low,
        attn_all[:, 2, :],
        down_pick[:, :, 2],
        up_pick[:, :, 2],
    )
    input_grad = (grad_from_query + grad_from_key + grad_from_value + grad_first).astype(
        jnp.bfloat16
    )
    down_terms = jnp.stack(
        (down_of_query, down_of_key, down_of_value, down_of_out, down_of_fc1), axis=2
    )
    up_terms = jnp.stack((up_of_query, up_of_key, up_of_value, up_of_out, up_of_fc2), axis=2)
    ff_terms = jnp.stack((up_of_fc1, down_of_fc2), axis=2)
    down_table = sum_by_adapter(onehot_full, down_terms)
    up_table = sum_by_adapter(onehot_full, up_terms)
    ff_table = sum_by_adapter(onehot_full, ff_terms)
    down_grad, up_grad, ff_grad = (
        lax.psum_scatter(down_table, ("fsdp", "seq"), scatter_dimension=0, tiled=True),
        lax.psum_scatter(up_table, ("fsdp", "seq"), scatter_dimension=0, tiled=True),
        lax.psum_scatter(ff_table, ("fsdp", "seq"), scatter_dimension=0, tiled=True),
    )
    return (layer_out, input_grad, down_grad, up_grad, ff_grad)


def solution(mesh):
    in_specs = (
        P("fsdp", "seq", None),
        P("fsdp", "seq", None),
        P("fsdp"),
        P("fsdp"),
        P(("fsdp", "seq"), None, None),
        P(("fsdp", "seq"), None),
        P(("fsdp", "seq"), None),
        P(("fsdp", "seq"), None),
        P(("fsdp", "seq")),
        P(("fsdp", "seq"), None, None, None),
        P(("fsdp", "seq"), None, None, None),
        P(("fsdp", "seq"), None, None, None),
    )
    out_specs = (
        P("fsdp", "seq", None),
        P("fsdp", "seq", None),
        P(("fsdp", "seq"), None, None, None),
        P(("fsdp", "seq"), None, None, None),
        P(("fsdp", "seq"), None, None, None),
    )
    return jax.shard_map(
        on_device, mesh=mesh, in_specs=in_specs, out_specs=out_specs, check_vma=False
    )
```

profile of v0, /device:TPU:0, one launch (start us, length us, event | category | flops | bytes accessed | tf_op | source)
XLA Modules:
  0.0 1272.0 jit_solution(4315957995622158347)
XLA Ops:
  13.6 87.2 %all-gather.13.cloned.1.call-done = bf16[1024,8,5,16]{3,1,2,0:T(8,128)(2,1)} async-done(((bf16[32,8,5,16]{3,1,2,0:T(8,128)(2,1)}), bf16[1024,8,5,16]{3,1,2,0:T(8,128)(2,1)}) %all-gather.13.cloned.1.call-update) | async-done | bytes 1310736 | tf_op jit(solution)/shard_map/all_gather | solution.py:213
  100.8 9.6 copy.133
  110.3 79.0 %all-gather.15.cloned.1.call-done = bf16[1024,8,5,16]{3,1,2,0:T(8,128)(2,1)} async-done(((bf16[32,8,5,16]{3,1,2,0:T(8,128)(2,1)}), bf16[1024,8,5,16]{3,1,2,0:T(8,128)(2,1)}) %all-gather.15.cloned.1.call-update) | async-done | bytes 1310736 | tf_op jit(solution)/shard_map/all_gather | solution.py:214
  189.4 9.6 copy.136
  202.0 66.8 %all-gather.11.cloned.1.call-done = bf16[1024,4,1024]{2,0,1:T(8,128)(2,1)} async-done(((bf16[32,4,1024]{2,0,1:T(8,128)(2,1)}), bf16[1024,4,1024]{2,0,1:T(8,128)(2,1)}) %all-gather.11.cloned.1.call-update) | async-done | bytes 8388624 | tf_op jit(solution)/shard_map/all_gather | solution.py:208
  272.0 39.5 %all-gather = bf16[32,32,8]{1,2,0:T(8,128)(2,1)S(1)} all-gather(bf16[1,32,8]{1,2,0:T(8,128)(2,1)S(1)} %bitcast.346), channel_id=1, replica_groups=mesh['fsdp'=2,'seq'=16] {'fsdp','seq'}, dimensions={0}, use_global_device_ids=true | all-gather | bytes 16896 | tf_op jit(solution)/shard_map/all_gather | solution.py:211
  317.1 36.5 %all-gather.1 = bf16[32,1,128]{2,1,0:T(2,128)(2,1)S(1)} all-gather(bf16[1,1,128]{2,1,0:T(2,128)(2,1)S(1)} %bitcast.347), channel_id=1, replica_groups=mesh['fsdp'=2,'seq'=16] {'fsdp','seq'}, dimensions={0}, use_global_device_ids=true | all-gather | bytes 8448 | tf_op jit(solution)/shard_map/all_gather | solution.py:212
  362.6 13.0 %all-gather.19.cloned.1.call-done = bf16[2,1024,1024]{2,1,0:T(8,128)(2,1)} async-done(((bf16[2,64,1024]{2,1,0:T(8,128)(2,1)}), bf16[2,1024,1024]{2,1,0:T(8,128)(2,1)}) %all-gather.19.cloned.1.call-update) | async-done | bytes 4194320 | tf_op jit(solution)/shard_map/all_gather | solution.py:231
  375.7 6.4 copy.146
  382.1 45.4 %all-gather.17.cloned.1.call-done = bf16[2,1024,1024]{2,1,0:T(8,128)(2,1)} async-done(((bf16[2,64,1024]{2,1,0:T(8,128)(2,1)}), bf16[2,1024,1024]{2,1,0:T(8,128)(2,1)}) %all-gather.17.cloned.1.call-update) | async-done | bytes 4194320 | tf_op jit(solution)/shard_map/all_gather | solution.py:232
  427.4 6.2 copy.145
  433.7 12.2 while.39
  446.4 22.5 %while.40 = (s32[]{:T(128)}, f32[2,64,16,64]{1,3,2,0:T(8,128)}, s32[2]{0:T(128)}, bf16[2,1024,1024]{1,2,0:T(8,128)(2,1)}, s32[2]{0:T(128)}, /*index=5*/bf16[2,10...) while((s32[]{:T(128)}, f32[2,64,16,64]{1,3,2,0:T(8,128)}, ...), condition=%wide.region_5.6_spmd.clone, body=%wide.region_4.5_spmd.clone.sunk | while | flops 271844864 | bytes 13908177 | solution.py:136
  449.6 3.9 constant_dynamic-slice_fusion.12
  453.5 4.0 fusion.222
  460.7 3.9 constant_dynamic-slice_fusion.12
  464.7 4.3 fusion.222
  475.6 30.7 %all-gather.21.cloned.1.call-done = bf16[1024,4096]{1,0:T(8,128)(2,1)} async-done(((bf16[32,4096]{1,0:T(8,128)(2,1)}), bf16[1024,4096]{1,0:T(8,128)(2,1)}) %all-gather.21.cloned.1.call-update) | async-done | bytes 8388624 | tf_op jit(solution)/shard_map/all_gather | solution.py:209
  506.3 4.8 fusion.21
  512.0 6.0 multiply_convert_fusion.1
  518.5 66.7 %all-gather.25.cloned.1.call-done = bf16[4096,1024]{1,0:T(8,128)(2,1)} async-done(((bf16[128,1024]{1,0:T(8,128)(2,1)}), bf16[4096,1024]{1,0:T(8,128)(2,1)}) %all-gather.25.cloned.1.call-update) | async-done | bytes 8388624 | tf_op jit(solution)/shard_map/all_gather | solution.py:210
  585.2 4.8 fusion.17
  592.4 2.9 fusion.15
  597.2 2.9 fusion.19
  601.6 2.4 fusion.36
  606.2 2.6 copy.201
  610.3 4.3 broadcast_in_dim.74.clone2
  614.6 4.2 broadcast_in_dim.74.clone
  618.8 57.9 %while.41 = (s32[]{:T(128)}, f32[2,64,16,64]{1,3,2,0:T(8,128)}, bf16[2,1024,1024]{2,0,1:T(2,128)(2,1)}, bf16[2,1024,1024]{2,0,1:T(2,128)(2,1)}, s32[2]{0:T(128)S...) while((s32[]{:T(128)}, f32[2,64,16,64]{1,3,2,0:T(8,128)}, ...), condition=%wide.region_15.16_spmd.clone, body=%wide.region_14.15_spmd.clone.sunk | while | flops 679740928 | bytes 77626696 | solution.py:178
  630.3 6.2 copy.301
  636.5 4.1 copy.300
  640.6 7.0 constant_dynamic-update-slice_fusion.3
  659.1 6.2 copy.301
  665.4 4.1 copy.300
  669.5 7.2 constant_dynamic-update-slice_fusion.3
  678.9 5.0 convolution_bitcast_fusion.1
  686.8 159.0 %all-reduce.5.cloned.1.call-done = (bf16[2,1024,1024]{2,0,1:T(2,128)(2,1)}, bf16[2,1024,1024]{2,0,1:T(2,128)(2,1)}) async-done(((bf16[2,1024,1024]{2,0,1:T(2,128)(2,1)}, bf16[2,1024,1024]{2,0,1:T(2,128)(2,1)}), (bf16[2,1024,1024]{2,0,1:T(2,128)(2,1)}, bf16[2,1024,1024]{2,0,1:T(2,128)(2,1)})) %all-reduce.5.cloned.1.call-update) | async-done | bytes 8388624
  850.5 3.1 convolution_bitcast_fusion.4
  853.6 19.4 %copy.208 = f32[1024,8,5,16]{1,3,2,0:T(8,128)} copy(f32[1024,8,5,16]{0,1,3,2:T(8,128)S(1)} %convolution_bitcast_fusion.4) | data formatting | bytes 5242880
  873.1 28.6 %reshape.257 = f32[1024,640]{1,0:T(8,128)} reshape(f32[1024,5,16,8]{3,2,1,0:T(8,128)} %bitcast.317) | data formatting | bytes 5242880
  906.0 19.4 %copy.206 = f32[1024,8,5,16]{1,3,2,0:T(8,128)} copy(f32[1024,8,5,16]{0,1,3,2:T(8,128)S(1)} %convolution_bitcast_fusion.5) | data formatting | bytes 5242880
  925.4 28.6 %reshape.255 = f32[1024,640]{1,0:T(8,128)} reshape(f32[1024,5,16,8]{3,2,1,0:T(8,128)} %bitcast.318) | data formatting | bytes 5242880
  954.0 2.5 fusion.34
  956.6 2.5 fusion.30
  959.4 2.5 fusion.32
  963.2 25.9 %reduce-scatter.8.cloned.1.call-done = f32[128,8,2,16]{0,1,3,2:T(8,128)} async-done(((f32[4096,8,2,16]{0,1,3,2:T(8,128)}), f32[128,8,2,16]{0,1,3,2:T(8,128)}) %reduce-scatter.8.cloned.1.call-update) | async-done | bytes 131088 | tf_op jit(solution)/shard_map/reduce_scatter | solution.py:333
  990.6 135.2 %reduce-scatter.12.cloned.1.call-done = f32[32,640]{1,0:T(8,128)} async-done(((f32[1024,640]{1,0:T(8,128)}), f32[32,640]{1,0:T(8,128)}) %reduce-scatter.12.cloned.1.call-update) | async-done | bytes 81936
  1128.8 133.0 %reduce-scatter.10.cloned.1.call-done = f32[32,640]{1,0:T(8,128)} async-done(((f32[1024,640]{1,0:T(8,128)}), f32[32,640]{1,0:T(8,128)}) %reduce-scatter.10.cloned.1.call-update) | async-done | bytes 81936
  (368 shorter events, 104.1 us)
Async XLA Ops:
  7.2 5.7 copy-start.70
  7.2 93.6 %all-gather.13.cloned.1.call-start = ((), (), s32[]{:S(2)}) async-start(), calls=%async_computation.4 | async-start | bytes 10813440 | tf_op jit(solution)/shard_map/all_gather | solution.py:213
  9.1 180.3 %all-gather.15.cloned.1.call-start = ((), (), s32[]{:S(2)}) async-start(), calls=%async_computation.5 | async-start | bytes 10813440 | tf_op jit(solution)/shard_map/all_gather | solution.py:214
  11.0 257.8 %all-gather.11.cloned.1.call-start = ((), (), s32[]{:S(2)}) async-start(), calls=%async_computation.3 | async-start | bytes 8650752 | tf_op jit(solution)/shard_map/all_gather | solution.py:208
  12.8 342.9 %all-gather.23.cloned.1.call-start = ((), (), s32[]{:S(2)}) async-start(), calls=%async_computation.9 | async-start | bytes 2162688 | tf_op jit(solution)/shard_map/all_gather | solution.py:215
  13.6 362.1 %all-gather.19.cloned.1.call-start = ((), (), s32[]{:S(2)}) async-start(), calls=%async_computation.7 | async-start | bytes 4456448 | tf_op jit(solution)/shard_map/all_gather | solution.py:231
  110.3 88.6 %copy-start.80 = (s32[2]{0:T(128)S(1)}, s32[2]{0:T(128)}, u32[]{:S(2)}) copy-start(s32[2]{0:T(128)} %param.21) | copy-start | bytes 28
  200.4 70.5 %copy-start.37 = (bf16[2,1024,16]{1,0,2:T(2,128)(2,1)}, bf16[2,1024,16]{1,0,2:T(2,128)(2,1)S(1)}, u32[]{:S(2)}) copy-start(bf16[2,1024,16]{1,0,2:T(2,128)(2,1)S(1)} %get-tuple-element.421) | copy-start | bytes 196612
  200.4 111.8 %copy-start.39 = (bf16[2,1024,16]{1,0,2:T(2,128)(2,1)}, bf16[2,1024,16]{1,0,2:T(2,128)(2,1)S(1)}, u32[]{:S(2)}) copy-start(bf16[2,1024,16]{1,0,2:T(2,128)(2,1)S(1)} %get-tuple-element.422) | copy-start | bytes 196612
  200.4 155.1 %copy-start.35 = (bf16[2,1024,16]{1,0,2:T(2,128)(2,1)}, bf16[2,1024,16]{1,0,2:T(2,128)(2,1)S(1)}, u32[]{:S(2)}) copy-start(bf16[2,1024,16]{1,0,2:T(2,128)(2,1)S(1)} %get-tuple-element.420) | copy-start | bytes 196612
  200.6 70.3 %copy-start.60 = (bf16[2,16,64]{2,1,0:T(8,128)(2,1)}, bf16[2,16,64]{2,1,0:T(8,128)(2,1)S(1)}, u32[]{:S(2)}) copy-start(bf16[2,16,64]{2,1,0:T(8,128)(2,1)S(1)} %convolution_convert_fusion.11) | copy-start | bytes 12292
  202.0 70.0 %copy-start.48 = (bf16[2,1024,16]{1,0,2:T(2,128)(2,1)}, bf16[2,1024,16]{1,0,2:T(2,128)(2,1)S(1)}, u32[]{:S(2)}) copy-start(bf16[2,1024,16]{1,0,2:T(2,128)(2,1)S(1)} %get-tuple-element.416) | copy-start | bytes 196612
  202.0 112.5 %copy-start.46 = (bf16[2,1024,16]{1,0,2:T(2,128)(2,1)}, bf16[2,1024,16]{1,0,2:T(2,128)(2,1)S(1)}, u32[]{:S(2)}) copy-start(bf16[2,1024,16]{1,0,2:T(2,128)(2,1)S(1)} %get-tuple-element.417) | copy-start | bytes 196612
  202.0 159.4 %copy-start.43 = (bf16[2,1024,16]{1,0,2:T(2,128)(2,1)}, bf16[2,1024,16]{1,0,2:T(2,128)(2,1)S(1)}, u32[]{:S(2)}) copy-start(bf16[2,1024,16]{1,0,2:T(2,128)(2,1)S(1)} %get-tuple-element.415) | copy-start | bytes 196612
  202.0 70.0 %copy-start.93 = (bf16[32,8]{0,1:T(8,128)(2,1)S(1)}, bf16[32,8]{0,1:T(8,128)(2,1)}, u32[]{:S(2)}) copy-start(bf16[32,8]{0,1:T(8,128)(2,1)} %param.25) | copy-start | bytes 1540
  271.9 155.6 %all-gather.17.cloned.1.call-start = ((), (), s32[]{:S(2)}) async-start(), calls=%async_computation.6 | async-start | bytes 4456448 | tf_op jit(solution)/shard_map/all_gather | solution.py:232
  312.3 43.4 %copy-start.81 = (s32[2]{0:T(128)S(1)}, s32[2]{0:T(128)}, u32[]{:S(2)}) copy-start(s32[2]{0:T(128)} %param.21) | copy-start | bytes 28
  315.4 190.8 %all-gather.21.cloned.1.call-start = ((), (), s32[]{:S(2)}) async-start(), calls=%async_computation.8 | async-start | bytes 8650752 | tf_op jit(solution)/shard_map/all_gather | solution.py:209
  316.2 269.0 %all-gather.25.cloned.1.call-start = ((), (), s32[]{:S(2)}) async-start(), calls=%async_computation.10 | async-start | bytes 8650752 | tf_op jit(solution)/shard_map/all_gather | solution.py:210
  317.0 528.8 %all-reduce.5.cloned.1.call-start = ((), (), s32[]{:S(2)}) async-start(), calls=%async_computation.14 | async-start | bytes 16777216
  355.7 5.7 copy-start.64
  506.3 4.8 copy-start.22
  506.3 4.8 copy-start.58
  506.3 4.8 copy-start.69
  512.0 6.0 copy-start.10
  512.0 6.0 copy-start.27
  518.0 72.0 %copy-start.5 = (bf16[2,64,4096]{2,1,0:T(8,128)(2,1)}, bf16[2,64,4096]{2,1,0:T(8,128)(2,1)S(1)}, u32[]{:S(2)}) copy-start(bf16[2,64,4096]{2,1,0:T(8,128)(2,1)S(1)} %get-tuple-element.401) | copy-start | bytes 3145732
  518.5 71.6 %copy-start.54 = (bf16[2,64,16]{1,2,0:T(8,128)(2,1)}, bf16[2,64,16]{1,2,0:T(8,128)(2,1)S(1)}, u32[]{:S(2)}) copy-start(bf16[2,64,16]{1,2,0:T(8,128)(2,1)S(1)} %convolution_convert_fusion.8) | copy-start | bytes 12292
  518.5 71.6 %copy-start.41 = (bf16[2,1024,16]{1,0,2:T(2,128)(2,1)S(1)}, bf16[2,1024,16]{1,0,2:T(2,128)(2,1)}, u32[]{:S(2)}) copy-start(bf16[2,1024,16]{1,0,2:T(2,128)(2,1)} %get-tuple-element.413) | copy-start | bytes 196612
  518.5 71.6 %copy-start.67 = (f32[1024,1]{0,1:T(1,128)S(1)}, f32[1024,1]{0,1:T(1,128)}, u32[]{:S(2)}) copy-start(f32[1024,1]{0,1:T(1,128)} %get-tuple-element.427) | copy-start | bytes 12292
  518.5 71.6 %copy-start.72 = (f32[2,64]{1,0:T(2,128)S(1)}, f32[2,64]{1,0:T(2,128)}, u32[]{:S(2)}) copy-start(f32[2,64]{1,0:T(2,128)} %copy-done.71) | copy-start | bytes 1540
  518.5 71.6 %copy-start.75 = (f32[1024,1]{0,1:T(1,128)S(1)}, f32[1024,1]{0,1:T(1,128)}, u32[]{:S(2)}) copy-start(f32[1024,1]{0,1:T(1,128)} %get-tuple-element.426) | copy-start | bytes 12292
  518.5 71.6 %copy-start.84 = (f32[1024,1]{0,1:T(1,128)S(1)}, f32[1024,1]{0,1:T(1,128)}, u32[]{:S(2)}) copy-start(f32[1024,1]{0,1:T(1,128)} %get-tuple-element.425) | copy-start | bytes 12292
  518.5 71.6 %copy-start.87 = (f32[2,64]{1,0:T(2,128)S(1)}, f32[2,64]{1,0:T(2,128)}, u32[]{:S(2)}) copy-start(f32[2,64]{1,0:T(2,128)} %copy-done.86) | copy-start | bytes 1540
  518.5 72.0 %copy-start.18 = (bf16[2,64,1024]{2,1,0:T(8,128)(2,1)S(1)}, bf16[2,64,1024]{2,1,0:T(8,128)(2,1)}, u32[]{:S(2)}) copy-start(bf16[2,64,1024]{2,1,0:T(8,128)(2,1)} %param.19) | copy-start | bytes 786436
  518.5 72.0 %copy-start.50 = (f32[1024,1]{0,1:T(1,128)S(1)}, f32[1024,1]{0,1:T(1,128)}, u32[]{:S(2)}) copy-start(f32[1024,1]{0,1:T(1,128)} %get-tuple-element.423) | copy-start | bytes 12292
  518.5 72.0 %copy-start.78 = (f32[2,64]{1,0:T(2,128)S(1)}, f32[2,64]{1,0:T(2,128)}, u32[]{:S(2)}) copy-start(f32[2,64]{1,0:T(2,128)} %compare_convert_fusion) | copy-start | bytes 1540
  585.2 7.1 copy-start.1
  591.2 5.9 slice-start
  676.7 312.3 %reduce-scatter.8.cloned.1.call-start = ((), (), s32[]{:S(2)}) async-start(), calls=%async_computation.11 | async-start | bytes 4325376 | tf_op jit(solution)/shard_map/reduce_scatter | solution.py:333
  683.9 163.3 %copy-start.61 = (bf16[2,16,64]{2,1,0:T(8,128)(2,1)S(1)}, bf16[2,16,64]{2,1,0:T(8,128)(2,1)}, u32[]{:S(2)}) copy-start(bf16[2,16,64]{2,1,0:T(8,128)(2,1)} %copy-done.60) | copy-start | bytes 12292
  683.9 164.1 %copy-start.63 = (bf16[2,16,64]{2,1,0:T(8,128)(2,1)S(1)}, bf16[2,16,64]{2,1,0:T(8,128)(2,1)}, u32[]{:S(2)}) copy-start(bf16[2,16,64]{2,1,0:T(8,128)(2,1)} %copy-done.62) | copy-start | bytes 12292
  683.9 164.9 %copy-start.25 = (bf16[2,64,1024]{2,1,0:T(8,128)(2,1)S(1)}, bf16[2,64,1024]{2,1,0:T(8,128)(2,1)}, u32[]{:S(2)}) copy-start(bf16[2,64,1024]{2,1,0:T(8,128)(2,1)} %copy-done.24) | copy-start | bytes 786436
  683.9 164.9 %copy-start.53 = (bf16[2,64,16]{1,2,0:T(8,128)(2,1)S(1)}, bf16[2,64,16]{1,2,0:T(8,128)(2,1)}, u32[]{:S(2)}) copy-start(bf16[2,64,16]{1,2,0:T(8,128)(2,1)} %copy-done.52) | copy-start | bytes 12292
  683.9 441.9 %reduce-scatter.12.cloned.1.call-start = ((), (), s32[]{:S(2)}) async-start(), calls=%async_computation.13 | async-start | bytes 2703360
  685.8 163.9 %copy-start.21 = (bf16[2,64,1024]{2,1,0:T(8,128)(2,1)S(1)}, bf16[2,64,1024]{2,1,0:T(8,128)(2,1)}, u32[]{:S(2)}) copy-start(bf16[2,64,1024]{2,1,0:T(8,128)(2,1)} %copy-done.20) | copy-start | bytes 786436
  685.8 163.9 %copy-start.55 = (bf16[2,64,16]{1,2,0:T(8,128)(2,1)S(1)}, bf16[2,64,16]{1,2,0:T(8,128)(2,1)}, u32[]{:S(2)}) copy-start(bf16[2,64,16]{1,2,0:T(8,128)(2,1)} %copy-done.54) | copy-start | bytes 12292
  901.7 360.1 %reduce-scatter.10.cloned.1.call-start = ((), (), s32[]{:S(2)}) async-start(), calls=%async_computation.12 | async-start | bytes 2703360
  (65 other events, 144.4 us)
Sparse Core Ops, SparseCore 0:
  11.5 89.2 all-gather.12
  104.3 85.0 all-gather.14
  192.9 75.9 all-gather.10
  271.5 51.8 all-gather.22
  326.1 49.5 all-gather.18
  378.3 49.1 all-gather.16
  430.3 75.9 all-gather.20
  509.1 76.0 all-gather.24
  676.8 168.8 all-reduce.4
  848.0 141.0 reduce-scatter.7
  991.4 134.3 reduce-scatter.11
  1128.1 133.6 reduce-scatter.9
where the time goes:
time: 1280 us; the launch traced here: 1270 us
  waiting for transfers between devices  843 us (66%)
  local copies, waits for them, and re-layouts  222 us (17%)
  matrix products  86.2 us (7%)
  blocking collectives  76 us (6%)
  other arithmetic  22.8 us (2%)
  between operations  16.7 us (1%)
    unnamed x15, waiting for transfers between devices  429 us
    unnamed x211, local copies, waits for them, and re-layouts  131 us
    all_gather x1, waiting for transfers between devices, on_device(): lax.all_gather(adapter_down, ('fsdp', 'seq'), axis=0, tiled=True)  87.2 us
    all_gather x1, waiting for transfers between devices, on_device(): lax.all_gather(adapter_up, ('fsdp', 'seq'), axis=0, tiled=True)  79 us
    all_gather x1, waiting for transfers between devices, on_device(): lax.all_gather(attn_weight, ('fsdp', 'seq'), axis=0, tiled=True)  66.8 us
    all_gather x1, waiting for transfers between devices, on_device(): lax.all_gather(fc2_weight, ('fsdp', 'seq'), axis=0, tiled=True)  66.7 us
    all_gather x1, waiting for transfers between devices, on_device(): lax.all_gather(values, 'seq', axis=1, tiled=True)  45.4 us
    all_gather x1, blocking collectives, on_device(): lax.all_gather(vectors, ('fsdp', 'seq'), axis=0, tiled=True)  39.5 us
  transfers between devices with their start and end apart: 12, of which 11 were waited for; matrix products, arithmetic and copies ran while one was open for 18% of the time, Pallas kernels for 0%

commit v1 on v0

--- a/solution.py
+++ b/solution.py
@@ -4,6 +4,8 @@
 import jax
 import jax.numpy as jnp
 from jax import lax
+from jax.experimental import pallas as pl
+from jax.experimental.pallas import tpu as pltpu
 from jax.sharding import PartitionSpec as P
 
 HEADS = 16
@@ -335,6 +337,760 @@
     return (layer_out, input_grad, down_grad, up_grad, ff_grad)
 
 
+MESH = pl.DeviceIdType.MESH
+CHUNKS = 14
+ROUTES = 11
+
+
+class Spot:
+    def __init__(self):
+        self.y = lax.axis_index("fsdp")
+        self.s = lax.axis_index("seq")
+        self.z = self.s // 4
+        self.x = (self.s // 2) % 2
+        self.c = self.s % 2
+
+    def at(self, dy=0, dz=0, dx=0, dc=0):
+        y = (self.y + dy) % 2
+        z = (self.z + dz) % 4
+        x = (self.x + dx) % 2
+        c = (self.c + dc) % 2
+        return (y, (z * 2 + x) * 2 + c)
+
+
+def enter(spot):
+    barrier = pltpu.get_barrier_semaphore()
+    for step in range(1, 16):
+        peer = (spot.y, (spot.s + step) % 16)
+        pl.semaphore_signal(barrier, inc=1, device_id=peer, device_id_type=MESH)
+    pl.semaphore_signal(barrier, inc=1, device_id=spot.at(dy=1), device_id_type=MESH)
+    pl.semaphore_wait(barrier, 16)
+
+
+class Gather:
+    def __init__(self, spot, parts, send, recv):
+        self.spot, self.parts, self.send, self.recv = spot, parts, send, recv
+        self.started = []
+
+    def block(self, k, dy, dx, dc, zs=slice(None)):
+        p = self.spot
+        if zs == slice(None):
+            zs = pl.ds(0, 4)
+        return self.parts[k].at[(p.y + dy) % 2, zs, (p.x + dx) % 2, (p.c + dc) % 2]
+
+    def piece(self, k, dz):
+        p = self.spot
+        return self.parts[k].at[p.y, (p.z + dz) % 4, p.x, p.c]
+
+    def copy(self, ref, k, route, peer):
+        return pltpu.make_async_remote_copy(
+            src_ref=ref,
+            dst_ref=ref,
+            send_sem=self.send.at[k, route],
+            recv_sem=self.recv.at[k, route],
+            device_id=peer,
+            device_id_type=MESH,
+        )
+
+    def push(self, ref, k, route, peer):
+        copy = self.copy(ref, k, route, peer)
+        copy.start()
+        self.started.append(copy)
+
+    def arrive(self, ref, k, route):
+        self.copy(ref, k, route, self.spot.at(dc=1)).wait_recv()
+
+    def along_z(self, k):
+        for d in range(1, 4):
+            self.push(self.piece(k, 0), k, d - 1, self.spot.at(dz=d))
+
+    def across(self, k):
+        for d in range(1, 4):
+            self.arrive(self.piece(k, 4 - d), k, d - 1)
+        line = self.block(k, 0, 0, 0)
+        self.push(line, k, 3, self.spot.at(dx=1))
+        self.push(line, k, 4, self.spot.at(dy=1))
+        self.push(line, k, 5, self.spot.at(dc=1))
+
+    def corner(self, k):
+        self.arrive(self.block(k, 0, 1, 0), k, 3)
+        self.push(self.block(k, 0, 1, 0, pl.ds(0, 2)), k, 6, self.spot.at(dy=1))
+        self.arrive(self.block(k, 1, 0, 0), k, 4)
+        self.push(self.block(k, 1, 0, 0, pl.ds(2, 2)), k, 7, self.spot.at(dx=1))
+        self.push(self.block(k, 0, 1, 0), k, 8, self.spot.at(dc=1))
+        self.push(self.block(k, 1, 0, 0), k, 9, self.spot.at(dc=1))
+
+    def twin(self, k):
+        self.arrive(self.block(k, 1, 1, 0, pl.ds(0, 2)), k, 6)
+        self.arrive(self.block(k, 1, 1, 0, pl.ds(2, 2)), k, 7)
+        self.push(self.block(k, 1, 1, 0), k, 10, self.spot.at(dc=1))
+
+    def ready(self, k):
+        self.arrive(self.block(k, 0, 0, 1), k, 5)
+        self.arrive(self.block(k, 0, 1, 1), k, 8)
+        self.arrive(self.block(k, 1, 0, 1), k, 9)
+        self.arrive(self.block(k, 1, 1, 1), k, 10)
+
+    def step(self, t):
+        for k, move in ((t, self.along_z), (t - 1, self.across), (t - 2, self.corner), (t - 3, self.twin)):
+            if 0 <= k < len(self.parts):
+                move(k)
+        if 0 <= t - 4 < len(self.parts):
+            self.ready(t - 4)
+
+    def finish(self):
+        for copy in self.started:
+            copy.wait_send()
+
+
+F32, BF16 = jnp.float32, jnp.bfloat16
+ORDER = (0, 12, 1, 2, 3, 13, 4, 5, 6, 7, 8, 9, 10, 11)
+EARLY, LATE = 96, 64
+
+
+def dot(left, right):
+    return jnp.dot(left, right, preferred_element_type=F32)
+
+
+def dot_nt(left, right):
+    return lax.dot_general(left, right, (((1,), (1,)), ((), ())), preferred_element_type=F32)
+
+
+def dot_tn(left, right):
+    return lax.dot_general(left, right, (((0,), (0,)), ((), ())), preferred_element_type=F32)
+
+
+def lanes(shape):
+    return lax.broadcasted_iota(jnp.int32, shape, len(shape) - 1)
+
+
+def half(value, slot):
+    low_half = lanes(value.shape) < HEAD
+    zero = jnp.zeros_like(value)
+    return jnp.where(low_half, value, zero) if slot == 0 else jnp.where(low_half, zero, value)
+
+
+def pair(first, second):
+    return jnp.where(lanes(first.shape) < HEAD, first, second)
+
+
+def swap(value):
+    return pltpu.roll(value, HEAD, 1)
+
+
+def rows_to_heads(rows, heads):
+    for p in range(HEADS // 2):
+        first = rows[0:64, p * 128 : p * 128 + 128]
+        second = rows[64:128, p * 128 : p * 128 + 128]
+        heads[2 * p] = pair(first, swap(second)).astype(BF16)
+        heads[2 * p + 1] = pair(swap(first), second).astype(BF16)
+
+
+def heads_to_rows(heads, rows, factor):
+    for p in range(HEADS // 2):
+        even = heads[2 * p].astype(F32) * factor
+        odd = heads[2 * p + 1].astype(F32) * factor
+        rows[0:64, p * 128 : p * 128 + 128] = pair(even, swap(odd)).astype(BF16)
+        rows[64:128, p * 128 : p * 128 + 128] = pair(swap(even), odd).astype(BF16)
+
+
+class Exchange:
+    def __init__(self, spot, out, into, send, recv):
+        self.spot, self.out, self.into, self.send, self.recv = spot, out, into, send, recv
+
+    def copy(self, unit, step, source, target, peer):
+        return pltpu.make_async_remote_copy(
+            src_ref=self.out.at[unit, source],
+            dst_ref=self.into.at[unit, target],
+            send_sem=self.send.at[unit, step],
+            recv_sem=self.recv.at[unit, step],
+            device_id=(self.spot.y, peer),
+            device_id_type=MESH,
+        )
+
+    def start(self, unit):
+        me = self.spot.s
+
+        def body(step, carry):
+            peer = (me + step) % 16
+            self.copy(unit, step, peer, me, peer).start()
+            return carry
+
+        lax.fori_loop(1, 16, body, 0)
+        self.into[unit, me] = self.out[unit, me]
+
+    def wait(self, unit):
+        me = self.spot.s
+
+        def body(step, carry):
+            peer = (me + 16 - step) % 16
+            self.copy(unit, step, peer, peer, peer).wait_recv()
+            return carry
+
+        lax.fori_loop(1, 16, body, 0)
+
+    def finish(self, units):
+        me = self.spot.s
+
+        def body(step, carry):
+            for unit in range(units):
+                self.copy(unit, step, (me + step) % 16, me, (me + step) % 16).wait_send()
+            return carry
+
+        lax.fori_loop(1, 16, body, 0)
+
+
+class Scatter:
+    def __init__(self, spot, own, core_in, core_sum, x_in, x_sum, z_in, z_sum, y_in, send, recv):
+        self.spot = spot
+        self.own, self.core_in, self.core_sum, self.x_in = own, core_in, core_sum, x_in
+        self.x_sum, self.z_in, self.z_sum, self.y_in = x_sum, z_in, z_sum, y_in
+        self.send, self.recv = send, recv
+        self.started = []
+
+    def push(self, source, target, route, peer):
+        copy = pltpu.make_async_remote_copy(
+            src_ref=source,
+            dst_ref=target,
+            send_sem=self.send.at[route],
+            recv_sem=self.recv.at[route],
+            device_id=peer,
+            device_id_type=MESH,
+        )
+        copy.start()
+        self.started.append(copy)
+
+    def first(self):
+        p = self.spot
+        self.push(self.own.at[:, :, :, 1 - p.c], self.core_in, 0, p.at(dc=1))
+
+    def second(self):
+        p = self.spot
+        self.started[0].wait_recv()
+        self.core_sum[...] = (self.own[:, :, :, p.c].astype(F32) + self.core_in[...].astype(F32)).astype(BF16)
+        self.push(self.core_sum.at[:, :, 1 - p.x], self.x_in, 1, p.at(dx=1))
+
+    def third(self):
+        p = self.spot
+        self.started[1].wait_recv()
+        self.x_sum[...] = (self.core_sum[:, :, p.x].astype(F32) + self.x_in[...].astype(F32)).astype(BF16)
+        for d in range(1, 4):
+            self.push(self.x_sum.at[:, (p.z + d) % 4], self.z_in.at[d - 1], 1 + d, p.at(dz=d))
+
+    def fourth(self, result):
+        p = self.spot
+        for d in range(1, 4):
+            self.started[1 + d].wait_recv()
+        total = self.x_sum[:, p.z].astype(F32)
+        for d in range(3):
+            total = total + self.z_in[d].astype(F32)
+        self.z_sum[...] = total.astype(BF16)
+        self.push(self.z_sum.at[1 - p.y], self.y_in, 5, p.at(dy=1))
+        result[p.y] = self.z_sum[p.y].astype(F32)
+
+    def fifth(self, result):
+        self.started[5].wait_recv()
+        result[1 - self.spot.y] = self.y_in[...].astype(F32)
+
+    def finish(self):
+        for copy in self.started:
+            copy.wait_send()
+
+
+def scatter_shapes(rows):
+    return [
+        pltpu.VMEM((2, 4, 2, 2, rows, 128), BF16),
+        pltpu.VMEM((2, 4, 2, rows, 128), BF16),
+        pltpu.VMEM((2, 4, 2, rows, 128), BF16),
+        pltpu.VMEM((2, 4, rows, 128), BF16),
+        pltpu.VMEM((2, 4, rows, 128), BF16),
+        pltpu.VMEM((3, 2, rows, 128), BF16),
+        pltpu.VMEM((2, rows, 128), BF16),
+        pltpu.VMEM((rows, 128), BF16),
+        pltpu.SemaphoreType.DMA((6,)),
+        pltpu.SemaphoreType.DMA((6,)),
+    ]
+
+
+def layer_kernel(*refs):
+    it = iter(refs)
+
+    def take(count):
+        return [next(it) for _ in range(count)]
+
+    attn, fc1, fc2, low_rank, ff_rank, tok, cot, lengths = take(8)
+    layer_out, input_grad, early_out, late_out = take(4)
+    wide, tall, rank_all, ff_all = take(4)
+    rank_in, rank_up, rank_x, vec, ff_low, bias = take(6)
+    heads_out, heads_in = take(2)
+    weights_low, weights_back = take(2)
+    tmp, attended, stat, sum_one, scaled_one, normed, scaled_two, grad_second, grad_first = take(9)
+    mixed, normed_low, out_low, branch_low, query_low, key_low, value_low = take(7)
+    slope, act, grad_hidden, inner4 = take(4)
+    early_refs, late_refs = take(10), take(10)
+    own, send, recv, hsend, hrecv = take(5)
+
+    spot = Spot()
+    here = (spot.y, spot.z, spot.x, spot.c)
+    parts = [wide.at[k] for k in range(8)] + [tall.at[k] for k in range(4)] + [rank_all, ff_all]
+    sources = [attn.at[j] for j in range(4)]
+    sources += [fc1.at[:, pl.ds(q * 1024, 1024)] for q in range(4)]
+    sources += [fc2.at[:, pl.ds(q * 256, 256)] for q in range(4)] + [low_rank, ff_rank]
+    placed = [pltpu.make_async_copy(sources[k], parts[k].at[here], own.at[k]) for k in ORDER]
+    for copy in placed:
+        copy.start()
+    gather = Gather(spot, [parts[k] for k in ORDER], send, recv)
+    swaps = Exchange(spot, heads_out, heads_in, hsend, hrecv)
+    early = Scatter(spot, *early_refs)
+    late = Scatter(spot, *late_refs)
+    enter(spot)
+    for copy in placed:
+        copy.wait()
+
+    lane = lanes((128, 128))
+    row_slot = lax.broadcasted_iota(jnp.int32, (128, 128), 0) >= 64
+    slot_lane = ((lane & 16) != 0) == row_slot
+    kind4 = [slot_lane & ((lane >> 5) == j) for j in range(4)]
+    kind_ff = [slot_lane & ((lane >> 5) == spot.y * 2 + k) for k in range(2)]
+
+    def only(mask, value):
+        return jnp.where(mask, value, jnp.zeros_like(value))
+
+    def square(k, t):
+        return wide[k, t // 2, pl.ds((t % 2) * 2, 2)].reshape(256, 1024)
+
+    def columns(k, cols):
+        return wide[k, :, :, :, :, :, cols].reshape(1024, 256)
+
+    def tile(n, size=256):
+        return pl.ds(pl.multiple_of(n * size, size), size)
+
+    def unpack_rank():
+        y_lanes = pl.ds(pl.multiple_of(spot.y * 128, 128), 128)
+        up_lanes = pl.ds(pl.multiple_of(spot.y * 128 + 256, 128), 128)
+        rank_in[...] = rank_all[:, :, :, :, :, y_lanes].reshape(1024, 128)
+        rank_up[...] = rank_all[:, :, :, :, :, up_lanes].reshape(1024, 128)
+        rank_x[...] = rank_all[:, :, :, :, :, 512:640].reshape(1024, 128)
+        vec[...] = rank_all[:, :, :, :, :, 640:768].reshape(1024, 128).astype(F32).T[0:8]
+
+    def unpack_ff():
+        ff_low[...] = ff_all[:, :, :, :, 0:128, :].reshape(4096, 128)
+        for o in range(32):
+            y, z, x, c = o // 16, (o // 4) % 4, (o // 2) % 2, o % 2
+            bias[:, o * 128 : o * 128 + 128] = ff_all[y, z, x, c, 128:136, :].astype(F32)
+
+    def project_in(j):
+        inner = only(kind4[j], inner4[...])
+
+        def body(n, carry):
+            cols = tile(n)
+            value = dot(tok[...], columns(j, cols)) + dot_nt(inner, rank_up[cols, :])
+            if j == 0:
+                value = (value + vec[0:1, cols]) * 0.125
+            if j == 2:
+                value = value + vec[1:2, cols]
+            tmp[:, cols] = value
+            return carry
+
+        lax.fori_loop(0, 4, body, 0)
+        rows_to_heads(tmp, heads_out.at[j])
+        swaps.start(j)
+
+    def attention():
+        for j in range(3):
+            swaps.wait(j)
+        keys = heads_in[1].reshape(1024, 128)
+        values = heads_in[2].reshape(1024, 128)
+
+        def body(t, carry):
+            rows = tile(t)
+            query = heads_in[0, pl.ds(t * 4, 4)].reshape(256, 128)
+            results, stats = [], []
+            for slot in range(2):
+                scores = dot_nt(half(query, slot), keys)
+                scores = jnp.where(lanes(scores.shape) < lengths[slot], scores, NEG_FILL)
+                top = jnp.max(scores, axis=-1, keepdims=True)
+                shifted = jnp.exp(scores - top)
+                total = jnp.sum(shifted, axis=-1, keepdims=True)
+                low = (shifted * (1.0 / total)).astype(BF16)
+                weights_low[slot, rows, :] = low
+                results.append(dot(low, values))
+                stats.append(jnp.broadcast_to(top + jnp.log(total), (256, 128)))
+            result = pair(results[0], results[1])
+            attended[rows, :] = result
+            heads_out[3, pl.ds(t * 4, 4)] = result.astype(BF16).reshape(4, 64, 128)
+            stat[rows, :] = pair(stats[0], stats[1])
+            return carry
+
+        lax.fori_loop(0, 4, body, 0)
+        swaps.start(3)
+
+    def attention_turned():
+        logsum = stat[...].T
+        queries = heads_in[0].reshape(1024, 128)
+        turned = [logsum[0:1], logsum[64:65]]
+
+        def body(t, carry):
+            rows = tile(t)
+            keys = heads_in[1, pl.ds(t * 4, 4)].reshape(256, 128)
+            for slot in range(2):
+                scores = dot_nt(half(keys, slot), queries)
+                weights = jnp.exp(scores - turned[slot])
+                place = lax.broadcasted_iota(jnp.int32, weights.shape, 0) + t * 256
+                weights = jnp.where(place < lengths[slot], weights, 0.0)
+                weights_back[slot, rows, :] = weights.astype(BF16)
+            return carry
+
+        lax.fori_loop(0, 4, body, 0)
+
+    def normalize(value):
+        centered = value - jnp.mean(value, axis=-1, keepdims=True)
+        spread = lax.rsqrt(jnp.mean(centered * centered, axis=-1, keepdims=True) + NORM_EPS)
+        return centered * spread, spread
+
+    def normalize_back(grad, scaled, spread):
+        shift = jnp.mean(grad, axis=-1, keepdims=True)
+        along = jnp.mean(grad * scaled, axis=-1, keepdims=True)
+        return spread * (grad - shift - scaled * along)
+
+    saved = {}
+
+    def branch():
+        swaps.wait(3)
+        heads_to_rows(heads_in.at[3], mixed, 1.0)
+        saved["o"] = only(kind4[3], dot(mixed[...], rank_in[...])).astype(BF16)
+
+        def body(n, carry):
+            cols = tile(n)
+            value = dot(mixed[...], columns(3, cols)) + dot_nt(saved["o"], rank_up[cols, :])
+            sum_one[:, cols] = tok[:, cols].astype(F32) + value + vec[2:3, cols]
+            return carry
+
+        lax.fori_loop(0, 4, body, 0)
+        scaled, saved["spread_one"] = normalize(sum_one[...])
+        scaled_one[...] = scaled
+        value = scaled * vec[4:5] + vec[5:6]
+        normed[...] = value
+        normed_low[...] = value.astype(BF16)
+        saved["hidden"] = only(kind_ff[0], dot(normed_low[...], rank_x[...])).astype(BF16)
+
+    def expand(q):
+        def body(n, carry):
+            cols = tile(n)
+            wide_cols = tile(q * 4 + n)
+            value = dot(normed_low[...], columns(4 + q, cols))
+            value = value + dot_nt(saved["hidden"], ff_low[wide_cols, :]) + bias[0:1, wide_cols]
+            share = 0.5 * (1.0 + lax.erf(value * math.sqrt(0.5)))
+            act[:, wide_cols] = (value * share).astype(BF16)
+            bell = jnp.exp(-0.5 * value * value) * (1.0 / math.sqrt(2.0 * math.pi))
+            slope[:, wide_cols] = share + value * bell
+            return carry
+
+        lax.fori_loop(0, 4, body, 0)
+
+    def contract(q):
+        if q == 0:
+            saved["out"] = only(kind_ff[1], dot(act[...], ff_low[...])).astype(BF16)
+        cols = pl.ds(q * 256, 256)
+        value = dot(act[...], tall[q].reshape(4096, 256)) + dot_nt(saved["out"], rank_x[cols, :])
+        tmp[:, cols] = normed[:, cols] + value + vec[3:4, cols]
+
+    def outer():
+        rows = lax.broadcasted_iota(jnp.int32, (128, 1), 0)
+        place = spot.s * 64 + (rows & 63)
+        limit = jnp.where(rows < 64, lengths[0], lengths[1])
+        live = (place < limit).astype(F32)
+        scaled, spread = normalize(tmp[...])
+        layer_out[...] = (live * (scaled * vec[6:7] + vec[7:8])).astype(BF16)
+        grad = normalize_back(live * cot[...].astype(F32) * vec[6:7], scaled, spread)
+        grad_second[...] = grad
+        out_low[...] = grad.astype(BF16)
+        saved["g_out"] = only(kind_ff[1], dot(out_low[...], rank_x[...])).astype(BF16)
+
+    def hidden_back():
+        def body(t, carry):
+            rows = tile(t, 512)
+            value = dot_nt(saved["g_out"], ff_low[rows, :])
+            for q in range(4):
+                piece = tall[q, t // 4, t % 4].reshape(512, 256)
+                value = value + dot_nt(out_low[:, q * 256 : q * 256 + 256], piece)
+            grad_hidden[:, rows] = (value * slope[:, rows]).astype(BF16)
+            return carry
+
+        lax.fori_loop(0, 8, body, 0)
+        saved["g_hidden"] = only(kind_ff[0], dot(grad_hidden[...], ff_low[...])).astype(BF16)
+
+    def normed_back():
+        def body(t, carry):
+            rows = tile(t)
+            value = dot_nt(saved["g_hidden"], rank_x[rows, :]) + grad_second[:, rows]
+            for q in range(4):
+                value = value + dot_nt(grad_hidden[:, q * 1024 : q * 1024 + 1024], square(4 + q, t))
+            tmp[:, rows] = value
+            return carry
+
+        lax.fori_loop(0, 4, body, 0)
+        grad = normalize_back(tmp[...] * vec[4:5], scaled_one[...], saved["spread_one"])
+        grad_first[...] = grad
+        branch_low[...] = grad.astype(BF16)
+        saved["g_o"] = only(kind4[3], dot(branch_low[...], rank_up[...])).astype(BF16)
+
+    def mixed_back():
+        def body(t, carry):
+            rows = tile(t)
+            tmp[:, rows] = dot_nt(branch_low[...], square(3, t)) + dot_nt(saved["g_o"], rank_in[rows, :])
+            return carry
+
+        lax.fori_loop(0, 4, body, 0)
+        rows_to_heads(tmp, heads_out.at[4])
+        swaps.start(4)
+
+    def early_grads():
+        own_grads = early.own
+        value = dot_tn(normed_low[...], saved["g_hidden"]) + dot_tn(out_low[...], saved["out"])
+        own_grads[:, :, :, :, 0:32, :] = value.astype(BF16).reshape(2, 4, 2, 2, 32, 128)
+        for y in range(2):
+            for z in range(4):
+                cols = slice((y * 4 + z) * 512, (y * 4 + z) * 512 + 512)
+                value = dot_tn(grad_hidden[:, cols], saved["hidden"]) + dot_tn(act[:, cols], saved["g_out"])
+                value = value.reshape(4, 128, 128)
+                for o in range(4):
+                    packed = value[o, 0:64] + swap(value[o, 64:128])
+                    own_grads[y, z, o // 2, o % 2, 32:96, :] = packed.astype(BF16)
+
+    def attention_back():
+        swaps.wait(4)
+        keys = heads_in[1].reshape(1024, 128)
+        values = heads_in[2].reshape(1024, 128)
+        queries = heads_in[0].reshape(1024, 128)
+        grads = heads_in[4].reshape(1024, 128)
+        product = grads.astype(F32) * attended[...]
+        deltas = [jnp.sum(half(product, slot), axis=-1, keepdims=True) for slot in range(2)]
+        stat[...] = pair(*[jnp.broadcast_to(delta, (1024, 128)) for delta in deltas])
+        turned = stat[...].T
+        turned = [turned[0:1], turned[64:65]]
+
+        def key_side(t, carry):
+            rows = tile(t)
+            value_block = heads_in[2, pl.ds(t * 4, 4)].reshape(256, 128)
+            key_parts, value_parts = [], []
+            for slot in range(2):
+                weights = weights_back[slot, rows, :]
+                grad_probs = dot_nt(half(value_block, slot), grads)
+                grad_scores = (weights.astype(F32) * (grad_probs - turned[slot])).astype(BF16)
+                key_parts.append(dot(grad_scores, queries))
+                value_parts.append(dot(weights, grads))
+            heads_out[6, pl.ds(t * 4, 4)] = pair(*key_parts).astype(BF16).reshape(4, 64, 128)
+            heads_out[7, pl.ds(t * 4, 4)] = pair(*value_parts).astype(BF16).reshape(4, 64, 128)
+            return carry
+
+        lax.fori_loop(0, 4, key_side, 0)
+        swaps.start(6)
+        swaps.start(7)
+
+        def query_side_block(t, carry):
+            rows = tile(t)
+            grad_block = heads_in[4, pl.ds(t * 4, 4)].reshape(256, 128)
+            delta_block = stat[rows, :]
+            query_parts = []
+            for slot in range(2):
+                grad_probs = dot_nt(half(grad_block, slot), values)
+                delta = delta_block[:, 64 * slot : 64 * slot + 1]
+                weights = weights_low[slot, rows, :].astype(F32)
+                grad_scores = (weights * (grad_probs - delta)).astype(BF16)
+                query_parts.append(dot(grad_scores, keys))
+            heads_out[5, pl.ds(t * 4, 4)] = pair(*query_parts).astype(BF16).reshape(4, 64, 128)
+            return carry
+
+        lax.fori_loop(0, 4, query_side_block, 0)
+        swaps.start(5)
+
+    def inputs_back():
+        swaps.wait(6)
+        heads_to_rows(heads_in.at[6], key_low, 1.0)
+        swaps.wait(7)
+        heads_to_rows(heads_in.at[7], value_low, 1.0)
+        swaps.wait(5)
+        heads_to_rows(heads_in.at[5], query_low, 0.125)
+        grads = (query_low, key_low, value_low)
+        inner = jnp.zeros((128, 128), F32)
+        for j in range(3):
+            inner = jnp.where(kind4[j], dot(grads[j][...], rank_up[...]), inner)
+        saved["g_in"] = inner.astype(BF16)
+        value = dot_tn(tok[...], saved["g_in"]) + dot_tn(mixed[...], saved["g_o"])
+        late.own[:, :, :, :, 0:32, :] = value.astype(BF16).reshape(2, 4, 2, 2, 32, 128)
+        value = dot_tn(branch_low[...], saved["o"])
+        for j in range(3):
+            value = value + dot_tn(grads[j][...], only(kind4[j], inner4[...]))
+        late.own[:, :, :, :, 32:64, :] = value.astype(BF16).reshape(2, 4, 2, 2, 32, 128)
+
+    def tokens_back(t):
+        rows = pl.ds(t * 256, 256)
+        value = dot_nt(saved["g_in"], rank_in[rows, :]) + grad_first[:, rows]
+        for j, grad in enumerate((query_low, key_low, value_low)):
+            value = value + dot_nt(grad[...], square(j, t))
+        input_grad[:, rows] = value.astype(BF16)
+
+    for t in range(CHUNKS + 4):
+        gather.step(t)
+        if t == 5:
+            unpack_rank()
+            inner4[...] = dot(tok[...], rank_in[...]).astype(BF16)
+        if 5 <= t <= 7:
+            project_in(t - 5)
+        if t == 9:
+            unpack_ff()
+            attention()
+        if t == 10:
+            attention_turned()
+        if t == 11:
+            branch()
+            expand(0)
+            expand(1)
+        if 12 <= t <= 13:
+            expand(t - 10)
+        if t >= 14:
+            contract(t - 14)
+    outer()
+    hidden_back()
+    normed_back()
+    mixed_back()
+    early_grads()
+    early.first()
+    early.second()
+    attention_back()
+    early.third()
+    early.fourth(early_out)
+    inputs_back()
+    late.first()
+    tokens_back(0)
+    late.second()
+    tokens_back(1)
+    tokens_back(2)
+    late.third()
+    tokens_back(3)
+    late.fourth(late_out)
+    early.fifth(early_out)
+    late.fifth(late_out)
+    gather.finish()
+    swaps.finish(8)
+    early.finish()
+    late.finish()
+
+
+def layer(attn, fc1, fc2, low_rank, ff_rank, tok, cot, lengths):
+    lead = (2, 4, 2, 2)
+    anywhere = pl.BlockSpec(memory_space=pl.ANY)
+    near = pl.BlockSpec(memory_space=pltpu.VMEM)
+    scalar = pl.BlockSpec(memory_space=pltpu.SMEM)
+
+    def buffer(*shape, dtype=BF16):
+        return pltpu.VMEM(shape, dtype)
+
+    scratch = [
+        buffer(8, *lead, 32, 1024),
+        buffer(4, *lead, 128, 256),
+        buffer(*lead, *low_rank.shape),
+        buffer(*lead, *ff_rank.shape),
+    ]
+    scratch += [buffer(1024, 128)] * 3 + [buffer(8, 1024, dtype=F32), buffer(4096, 128)]
+    scratch += [buffer(8, 4096, dtype=F32)]
+    scratch += [buffer(8, 16, 64, 128)] * 2
+    scratch += [buffer(2, 1024, 1024)] * 2
+    scratch += [buffer(128, 1024, dtype=F32)] + [buffer(1024, 128, dtype=F32)] * 2
+    scratch += [buffer(128, 1024, dtype=F32)] * 6
+    scratch += [buffer(128, 1024)] * 7
+    scratch += [buffer(128, 4096, dtype=F32), buffer(128, 4096), buffer(128, 4096), buffer(128, 128)]
+    scratch += scatter_shapes(EARLY) + scatter_shapes(LATE)
+    scratch += [pltpu.SemaphoreType.DMA((CHUNKS,))]
+    scratch += [pltpu.SemaphoreType.DMA((CHUNKS, ROUTES))] * 2
+    scratch += [pltpu.SemaphoreType.DMA((8, 16))] * 2
+    return pl.pallas_call(
+        layer_kernel,
+        out_shape=[
+            jax.ShapeDtypeStruct(tok.shape, BF16),
+            jax.ShapeDtypeStruct(tok.shape, BF16),
+            jax.ShapeDtypeStruct((2, EARLY, 128), F32),
+            jax.ShapeDtypeStruct((2, LATE, 128), F32),
+        ],
+        in_specs=[anywhere] * 5 + [near] * 2 + [scalar],
+        out_specs=[near] * 4,
+        scratch_shapes=scratch,
+        compiler_params=pltpu.CompilerParams(
+            collective_id=0, has_side_effects=True, vmem_limit_bytes=63 * 2**20
+        ),
+        name="layer",
+    )(attn, fc1, fc2, low_rank, ff_rank, tok, cot, lengths)
+
+
+def fast_device(
+    tokens,
+    cotangent,
+    lengths,
+    adapter_ids,
+    attn_weight,
+    fc1_weight,
+    fc2_weight,
+    vectors,
+    fc1_bias,
+    adapter_down,
+    adapter_up,
+    ff_adapters,
+):
+    rows, width = adapter_down.shape[0], tokens.shape[2]
+    ff_rows = ff_adapters.shape[0]
+    ids = lax.all_gather(adapter_ids, "fsdp", axis=0, tiled=True)
+    onehot = ids[:, None] == jnp.arange(ADAPTERS)[None, :]
+
+    def pick(table):
+        picked = jnp.einsum("si,dikr->dskr", onehot.astype(BF16), table, preferred_element_type=F32)
+        picked = picked.astype(BF16).reshape(table.shape[0], 2, 2, table.shape[2], 16)
+        return picked.transpose(0, 1, 3, 2, 4)
+
+    down, up, ff_part = pick(adapter_down), pick(adapter_up), pick(ff_adapters)
+    cross = jnp.stack([down[:, :, 4], up[:, :, 4]], axis=2)
+    low_rank = jnp.concatenate(
+        [
+            down[:, :, :4].reshape(rows, 256),
+            up[:, :, :4].reshape(rows, 256),
+            cross.reshape(rows, 128),
+            jnp.pad(vectors, ((0, 0), (0, 120))),
+        ],
+        axis=1,
+    )
+    bias_rows = jnp.broadcast_to(fc1_bias[None], (16, ff_rows))
+    ff_rank = jnp.concatenate([ff_part.reshape(ff_rows, 128), bias_rows], axis=0)
+    layer_out, input_grad, early, late = layer(
+        attn_weight.transpose(1, 0, 2),
+        fc1_weight,
+        fc2_weight,
+        low_rank,
+        ff_rank,
+        tokens.reshape(-1, width),
+        cotangent.reshape(-1, width),
+        lengths,
+    )
+    picks = onehot.astype(F32).reshape(2, 2, ADAPTERS)
+    four = late.reshape(2, 2, rows, 4, 2, 16)
+    cross = early[:, :rows].reshape(2, rows, 2, 64)
+    cross = jnp.stack([cross[0, :, 0], cross[1, :, 1]]).reshape(2, rows, 2, 2, 16)
+    packed = early[:, rows:]
+    ff_first = jnp.concatenate([packed[0, :, :64], packed[0, :, 64:]], axis=0)
+    ff_second = jnp.concatenate([packed[1, :, 64:], packed[1, :, :64]], axis=0)
+    ff_terms = jnp.stack([ff_first, ff_second]).reshape(2, ff_rows, 2, 2, 16)
+
+    def spread(terms):
+        return jnp.einsum("ysi,ydksr->dikr", picks, terms, precision=lax.Precision.HIGHEST)
+
+    return (
+        layer_out.reshape(tokens.shape),
+        input_grad.reshape(tokens.shape),
+        spread(jnp.concatenate([four[:, 0], cross[:, :, 0:1]], axis=2)),
+        spread(jnp.concatenate([four[:, 1], cross[:, :, 1:2]], axis=2)),
+        spread(ff_terms),
+    )
+
+
 def solution(mesh):
     in_specs = (
         P("fsdp", "seq", None),
@@ -357,6 +1113,7 @@
         P(("fsdp", "seq"), None, None, None),
         P(("fsdp", "seq"), None, None, None),
     )
+    fast = mesh.shape["fsdp"] == 2 and mesh.shape["seq"] == HEADS
     return jax.shard_map(
-        on_device, mesh=mesh, in_specs=in_specs, out_specs=out_specs, check_vma=False
-    )
+        fast_device if fast else on_device, mesh=mesh, in_specs=in_specs, out_specs=out_specs, check_vma=False
+    )

time: 1280 us -> 235 us (0.18)
  waiting for transfers between devices: 843 us -> 0 us
  Pallas kernels: 0 us -> 212 us
  local copies, waits for them, and re-layouts: 222 us -> 12.5 us
  matrix products: 86.2 us -> 2.02 us
  blocking collectives: 76 us -> 5.22 us
  other arithmetic: 22.8 us -> 1.31 us
  between operations: 16.7 us -> 1.56 us
    unnamed x15 -> x0, waiting for transfers between devices: 429 us -> none
    all_gather x8 -> x0, waiting for transfers between devices: 389 us -> none  [the longest x1 87.2 us: on_device(): lax.all_gather(adapter_down, ('fsdp', 'seq'), axis=0, tiled=True)]
    pallas_call x0 -> x1, Pallas kernels: none -> 212 us  [layer(): pl.pallas_call(layer_kernel, out_shape=[jax.ShapeDtypeStruct(tok.shape, B...]
    unnamed x211 -> x32, local copies, waits for them, and re-layouts: 131 us -> 9.72 us
    dot_general x68 -> x6, matrix products: 86.2 us -> 2.02 us  [the longest x3 1.32 us: spread(): jnp.einsum('ysi,ydksr->dikr', picks, terms, precision=lax.Precision.HIGHEST)]
    all_gather x2 -> x0, blocking collectives: 76 us -> none  [the longest x1 39.5 us: on_device(): lax.all_gather(vectors, ('fsdp', 'seq'), axis=0, tiled=True)]
    dynamic_update_slice x6 -> x0, local copies, waits for them, and re-layouts: 34.9 us -> none  [the longest x4 22.5 us: step(): lax.dynamic_update_slice_in_dim(running[2], value_part, offset, 1)]
    reduce_scatter x1 -> x0, waiting for transfers between devices: 25.9 us -> none  [on_device(): lax.psum_scatter(ff_table, ('fsdp', 'seq'), scatter_dimension=0, tiled=True)]
  transfers between devices with their start and end apart: 12 -> 0, of which waited for: 11 -> 0; matrix products, arithmetic and copies ran while one was open for 18% -> 0% of each run, Pallas kernels for 0% -> 0%
where the time goes in v1:
time: 235 us; the launch traced here: 234 us
  Pallas kernels  212 us (90%)
  local copies, waits for them, and re-layouts  12.5 us (5%)
  blocking collectives  5.22 us (2%)
    pallas_call x1, Pallas kernels, layer(): pl.pallas_call(layer_kernel, out_shape=[jax.ShapeDtypeStruct(tok.shape, B...  212 us
    unnamed x32, local copies, waits for them, and re-layouts  9.72 us
    unnamed x1, blocking collectives  5.22 us

profile of v1, /device:TPU:0, one launch (start us, length us, event | category | flops | bytes accessed | tf_op | source)
XLA Modules:
  0.0 234.1 jit_solution(13044164945345843927)
XLA Ops:
  0.6 0.0 copy-start
  0.6 0.0 copy-start.7
  0.7 1.8 copy.85
  2.4 0.1 copy.40
  2.5 0.7 copy-done.10
  3.2 0.6 dynamic-slice
  4.4 0.0 copy-start.9
  4.4 0.6 copy-done.9
  5.1 0.2 dynamic-update-slice
  5.3 5.2 %all-reduce.1 = s32[4]{0:T(128)S(1)} all-reduce(s32[4]{0:T(128)S(1)} %dynamic-update-slice), channel_id=1, replica_groups=mesh['fsdp'=2,'seq'=16] {'fsdp'}, use_global_device_ids=true, to_apply=%add.1 | all-reduce | flops 4 | bytes 32
  10.5 0.2 convolution_convert_fusion
  10.8 0.6 copy-done.4
  11.4 0.2 convolution_convert_fusion.1
  11.7 0.1 copy.43
  11.8 0.1 copy.42
  11.9 0.1 copy.41
  12.0 0.0 copy-start.6
  12.0 0.6 fusion.24.refs_3_
  12.6 0.0 copy-done.8
  12.6 0.2 copy-done.6
  12.9 0.2 convolution_convert_fusion.2
  13.1 0.1 copy.46
  13.2 0.6 pad_maximum_fusion.refs_4_
  13.8 211.5 %layer.1 = (bf16[128,1024]{1,0:T(8,128)(2,1)}, bf16[128,1024]{1,0:T(8,128)(2,1)}, f32[2,96,128]{2,1,0:T(8,128)}, f32[2,64,128]{2,1,0:T(8,128)}) custom-call(bf16[4,32,1024]{2,1,0:T(8,128)(2,1)} %bitcast.73, bf16[32,4096]{1,0:T(8,128)(2,1)} %refs_1_.1, bf16[128,1024]{1,0:T(8,128)(2,1)} %refs_2_.1, bf16[32,768]{1,0:T(8,128)(2,1)} %fusion.24.refs_3_, ...), custom_call_target="tpu_custom_call" | custom-call | tf_op jit(solution)/shard_map/layer/pallas_call | solution.py:1008
  225.3 0.8 slice.55
  226.1 0.1 copy.71
  226.4 0.8 copy-done.5
  227.2 0.1 copy.47
  227.3 0.2 reshape.88
  227.5 0.2 fusion.40
  227.7 0.2 copy_bitcast_fusion.1
  227.9 0.1 eq.25
  228.0 0.1 copy.53
  228.1 0.4 convolution_bitcast_fusion.1
  228.5 0.8 copy.63
  229.3 0.5 convolution_bitcast_fusion
  229.8 0.8 copy.64
  230.6 0.1 copy-done.1
  230.7 0.1 fusion.42
  230.8 0.1 copy.60
  230.9 0.1 copy.59
  231.0 0.1 copy.56
  231.2 0.1 copy.55
  231.3 0.4 convolution_bitcast_fusion.2
  231.7 0.7 copy.65
  232.4 0.7 copy.91
  233.1 0.3 copy-done.2
  233.4 0.7 copy.92
  (28 shorter events, 0.4 us)
Async XLA Ops:
  0.6 9.8 %copy-start = (bf16[32,8,5,16]{0,3,2,1:T(8,128)(2,1)S(1)}, bf16[32,8,5,16]{0,3,2,1:T(8,128)(2,1)}, u32[]{:S(2)}) copy-start(bf16[32,8,5,16]{0,3,2,1:T(8,128)(2,1)} %param.22) | copy-start | bytes 122884
  0.6 1.8 copy-start.7
  2.5 0.7 copy-start.10
  4.4 0.7 copy-start.9
  10.5 0.9 copy-start.4
  12.0 0.7 copy-start.8
  12.0 0.9 copy-start.6
  226.3 0.8 copy-start.5
  229.8 0.9 copy-start.1
  231.3 1.1 copy-start.3
  232.4 1.0 copy-start.2

commit v2 on v1

--- a/solution.py
+++ b/solution.py
@@ -338,8 +338,9 @@
 
 
 MESH = pl.DeviceIdType.MESH
-CHUNKS = 14
+CHUNKS = 26
 ROUTES = 11
+ALL2, ALL4 = pl.ds(0, 2), pl.ds(0, 4)
 
 
 class Spot:
@@ -368,75 +369,94 @@
 
 
 class Gather:
-    def __init__(self, spot, parts, send, recv):
-        self.spot, self.parts, self.send, self.recv = spot, parts, send, recv
+    def __init__(self, spot, parts, ways, others, send, recv):
+        self.spot, self.parts, self.ways, self.others = spot, parts, ways, others
+        self.send, self.recv = send, recv
         self.started = []
 
-    def block(self, k, dy, dx, dc, zs=slice(None)):
+    def block(self, k, dy=0, dz=0, dx=0, dc=0):
         p = self.spot
-        if zs == slice(None):
-            zs = pl.ds(0, 4)
-        return self.parts[k].at[(p.y + dy) % 2, zs, (p.x + dx) % 2, (p.c + dc) % 2]
-
-    def piece(self, k, dz):
-        p = self.spot
-        return self.parts[k].at[p.y, (p.z + dz) % 4, p.x, p.c]
-
-    def copy(self, ref, k, route, peer):
+        places = ((p.y, dy, 2), (p.z, dz, 4), (p.x, dx, 2), (p.c, dc, 2))
+        return self.parts[k].at[tuple((place + d) % n if isinstance(d, int) else d for place, d, n in places)]
+
+    def copy(self, source, target, k, route, peer):
         return pltpu.make_async_remote_copy(
-            src_ref=ref,
-            dst_ref=ref,
+            src_ref=source,
+            dst_ref=target,
             send_sem=self.send.at[k, route],
             recv_sem=self.recv.at[k, route],
             device_id=peer,
             device_id_type=MESH,
         )
 
-    def push(self, ref, k, route, peer):
-        copy = self.copy(ref, k, route, peer)
+    def push(self, ref, k, route, source=None, **hop):
+        copy = self.copy(ref if source is None else source, ref, k, route, self.spot.at(**hop))
         copy.start()
         self.started.append(copy)
 
     def arrive(self, ref, k, route):
-        self.copy(ref, k, route, self.spot.at(dc=1)).wait_recv()
-
-    def along_z(self, k):
-        for d in range(1, 4):
-            self.push(self.piece(k, 0), k, d - 1, self.spot.at(dz=d))
-
-    def across(self, k):
-        for d in range(1, 4):
-            self.arrive(self.piece(k, 4 - d), k, d - 1)
-        line = self.block(k, 0, 0, 0)
-        self.push(line, k, 3, self.spot.at(dx=1))
-        self.push(line, k, 4, self.spot.at(dy=1))
-        self.push(line, k, 5, self.spot.at(dc=1))
-
-    def corner(self, k):
-        self.arrive(self.block(k, 0, 1, 0), k, 3)
-        self.push(self.block(k, 0, 1, 0, pl.ds(0, 2)), k, 6, self.spot.at(dy=1))
-        self.arrive(self.block(k, 1, 0, 0), k, 4)
-        self.push(self.block(k, 1, 0, 0, pl.ds(2, 2)), k, 7, self.spot.at(dx=1))
-        self.push(self.block(k, 0, 1, 0), k, 8, self.spot.at(dc=1))
-        self.push(self.block(k, 1, 0, 0), k, 9, self.spot.at(dc=1))
-
-    def twin(self, k):
-        self.arrive(self.block(k, 1, 1, 0, pl.ds(0, 2)), k, 6)
-        self.arrive(self.block(k, 1, 1, 0, pl.ds(2, 2)), k, 7)
-        self.push(self.block(k, 1, 1, 0), k, 10, self.spot.at(dc=1))
+        self.copy(ref, ref, k, route, self.spot.at(dc=1)).wait_recv()
+
+    def first(self, k):
+        if self.ways[k] == "z":
+            for d in range(1, 4):
+                self.push(self.block(k), k, d - 1, dz=d)
+        else:
+            self.push(self.block(k), k, 0, self.others.get(k), **{"d" + self.ways[k]: 1})
+
+    def second(self, k):
+        if self.ways[k] == "z":
+            for d in range(1, 4):
+                self.arrive(self.block(k, dz=4 - d), k, d - 1)
+            line = self.block(k, dz=ALL4)
+            self.push(line, k, 3, dx=1)
+            self.push(line, k, 4, dy=1)
+            self.push(line, k, 5, dc=1)
+        else:
+            self.arrive(self.block(k, **{"d" + self.ways[k]: 1}), k, 0)
+            for d in range(1, 4):
+                self.push(self.block(k, **{"d" + self.ways[k]: ALL2}), k, d, dz=d)
+
+    def third(self, k):
+        if self.ways[k] == "z":
+            self.arrive(self.block(k, dz=ALL4, dx=1), k, 3)
+            self.push(self.block(k, dz=pl.ds(0, 2), dx=1), k, 6, dy=1)
+            self.arrive(self.block(k, dz=ALL4, dy=1), k, 4)
+            self.push(self.block(k, dz=pl.ds(2, 2), dy=1), k, 7, dx=1)
+            self.push(self.block(k, dz=ALL4, dx=1), k, 8, dc=1)
+            self.push(self.block(k, dz=ALL4, dy=1), k, 9, dc=1)
+        else:
+            near, far = "d" + self.ways[k], "dy" if self.ways[k] == "x" else "dx"
+            for d in range(1, 4):
+                self.arrive(self.block(k, **{near: ALL2, "dz": 4 - d}), k, d)
+            plane = self.block(k, **{near: ALL2, "dz": ALL4})
+            self.push(plane, k, 4, **{far: 1})
+            self.push(plane, k, 5, dc=1)
+
+    def fourth(self, k):
+        if self.ways[k] == "z":
+            self.arrive(self.block(k, dz=pl.ds(0, 2), dx=1, dy=1), k, 6)
+            self.arrive(self.block(k, dz=pl.ds(2, 2), dx=1, dy=1), k, 7)
+            self.push(self.block(k, dz=ALL4, dx=1, dy=1), k, 10, dc=1)
+        else:
+            near, far = "d" + self.ways[k], "dy" if self.ways[k] == "x" else "dx"
+            plane = self.block(k, **{near: ALL2, "dz": ALL4, far: 1})
+            self.arrive(plane, k, 4)
+            self.push(plane, k, 6, dc=1)
 
     def ready(self, k):
-        self.arrive(self.block(k, 0, 0, 1), k, 5)
-        self.arrive(self.block(k, 0, 1, 1), k, 8)
-        self.arrive(self.block(k, 1, 0, 1), k, 9)
-        self.arrive(self.block(k, 1, 1, 1), k, 10)
+        if self.ways[k] == "z":
+            for route, dx, dy in ((5, 0, 0), (8, 1, 0), (9, 0, 1), (10, 1, 1)):
+                self.arrive(self.block(k, dz=ALL4, dx=dx, dy=dy, dc=1), k, route)
+        else:
+            near, far = "d" + self.ways[k], "dy" if self.ways[k] == "x" else "dx"
+            for route in range(2):
+                self.arrive(self.block(k, **{near: ALL2, "dz": ALL4, far: route, "dc": 1}), k, 5 + route)
 
     def step(self, t):
-        for k, move in ((t, self.along_z), (t - 1, self.across), (t - 2, self.corner), (t - 3, self.twin)):
-            if 0 <= k < len(self.parts):
-                move(k)
-        if 0 <= t - 4 < len(self.parts):
-            self.ready(t - 4)
+        for late, move in enumerate((self.first, self.second, self.third, self.fourth, self.ready)):
+            if 0 <= t - late < len(self.parts):
+                move(t - late)
 
     def finish(self):
         for copy in self.started:
@@ -444,8 +464,9 @@
 
 
 F32, BF16 = jnp.float32, jnp.bfloat16
-ORDER = (0, 12, 1, 2, 3, 13, 4, 5, 6, 7, 8, 9, 10, 11)
-EARLY, LATE = 96, 64
+ORDER = (0, 1, 24, 25) + tuple(range(2, 24))
+WAYS = "zzyyzzzzzzzzzzzzzzzzzzzzzz"
+EARLY, LATE = 80, 64
 
 
 def dot(left, right):
@@ -476,14 +497,6 @@
 
 def swap(value):
     return pltpu.roll(value, HEAD, 1)
-
-
-def rows_to_heads(rows, heads):
-    for p in range(HEADS // 2):
-        first = rows[0:64, p * 128 : p * 128 + 128]
-        second = rows[64:128, p * 128 : p * 128 + 128]
-        heads[2 * p] = pair(first, swap(second)).astype(BF16)
-        heads[2 * p + 1] = pair(swap(first), second).astype(BF16)
 
 
 def heads_to_rows(heads, rows, factor):
@@ -508,16 +521,36 @@
             device_id_type=MESH,
         )
 
-    def start(self, unit):
+    def start(self, unit, block):
         me = self.spot.s
 
-        def body(step, carry):
-            peer = (me + step) % 16
-            self.copy(unit, step, peer, me, peer).start()
+        def body(i, carry):
+            peer = block * 4 + i
+
+            @pl.when(peer != me)
+            def _():
+                self.copy(unit, (peer + 16 - me) % 16, peer, me, peer).start()
+
             return carry
 
-        lax.fori_loop(1, 16, body, 0)
-        self.into[unit, me] = self.out[unit, me]
+        lax.fori_loop(0, 4, body, 0)
+
+    def keep(self, unit):
+        self.into[unit, self.spot.s] = self.out[unit, self.spot.s]
+
+    def wait_block(self, unit, block):
+        me = self.spot.s
+
+        def body(i, carry):
+            peer = block * 4 + i
+
+            @pl.when(peer != me)
+            def _():
+                self.copy(unit, (me + 16 - peer) % 16, peer, peer, peer).wait_recv()
+
+            return carry
+
+        lax.fori_loop(0, 4, body, 0)
 
     def wait(self, unit):
         me = self.spot.s
@@ -541,14 +574,15 @@
 
 
 class Scatter:
-    def __init__(self, spot, own, core_in, core_sum, x_in, x_sum, z_in, z_sum, y_in, send, recv):
-        self.spot = spot
-        self.own, self.core_in, self.core_sum, self.x_in = own, core_in, core_sum, x_in
-        self.x_sum, self.z_in, self.z_sum, self.y_in = x_sum, z_in, z_sum, y_in
+    def __init__(self, spot, wide, own, core_in, core_sum, x_in, x_sum, into, send, recv):
+        self.spot, self.wide = spot, wide
+        self.own, self.core_in, self.core_sum = own, core_in, core_sum
+        self.x_in, self.x_sum, self.into = x_in, x_sum, into
         self.send, self.recv = send, recv
         self.started = []
 
-    def push(self, source, target, route, peer):
+    def push(self, source, target, peer):
+        route = len(self.started)
         copy = pltpu.make_async_remote_copy(
             src_ref=source,
             dst_ref=target,
@@ -562,53 +596,59 @@
 
     def first(self):
         p = self.spot
-        self.push(self.own.at[:, :, :, 1 - p.c], self.core_in, 0, p.at(dc=1))
+        self.push(self.own.at[:, :, :, 1 - p.c], self.core_in, p.at(dc=1))
 
     def second(self):
         p = self.spot
         self.started[0].wait_recv()
         self.core_sum[...] = (self.own[:, :, :, p.c].astype(F32) + self.core_in[...].astype(F32)).astype(BF16)
-        self.push(self.core_sum.at[:, :, 1 - p.x], self.x_in, 1, p.at(dx=1))
+        if not self.wide:
+            self.push(self.core_sum.at[:, :, 1 - p.x], self.x_in, p.at(dx=1))
 
     def third(self):
         p = self.spot
-        self.started[1].wait_recv()
-        self.x_sum[...] = (self.core_sum[:, :, p.x].astype(F32) + self.x_in[...].astype(F32)).astype(BF16)
-        for d in range(1, 4):
-            self.push(self.x_sum.at[:, (p.z + d) % 4], self.z_in.at[d - 1], 1 + d, p.at(dz=d))
-
-    def fourth(self, result):
+        if not self.wide:
+            self.started[1].wait_recv()
+            self.x_sum[...] = (self.core_sum[:, :, p.x].astype(F32) + self.x_in[...].astype(F32)).astype(BF16)
+        for dy in range(2):
+            for dz in range(4):
+                for dx in range(2 if self.wide else 1):
+                    if dy + dz + dx == 0:
+                        continue
+                    y, z, x = (p.y + dy) % 2, (p.z + dz) % 4, (p.x + dx) % 2
+                    source = self.core_sum.at[y, z, x] if self.wide else self.x_sum.at[y, z]
+                    self.push(source, self.into.at[dy, dz, dx], p.at(dy=dy, dz=dz, dx=dx))
+
+    def fourth(self):
         p = self.spot
-        for d in range(1, 4):
-            self.started[1 + d].wait_recv()
-        total = self.x_sum[:, p.z].astype(F32)
-        for d in range(3):
-            total = total + self.z_in[d].astype(F32)
-        self.z_sum[...] = total.astype(BF16)
-        self.push(self.z_sum.at[1 - p.y], self.y_in, 5, p.at(dy=1))
-        result[p.y] = self.z_sum[p.y].astype(F32)
-
-    def fifth(self, result):
-        self.started[5].wait_recv()
-        result[1 - self.spot.y] = self.y_in[...].astype(F32)
+        for copy in self.started[1 if self.wide else 2 :]:
+            copy.wait_recv()
+        total = [self.core_sum[p.y, p.z, p.x] if self.wide else self.x_sum[p.y, p.z], None]
+        total[0] = total[0].astype(F32)
+        for dy in range(2):
+            for dz in range(4):
+                for dx in range(2 if self.wide else 1):
+                    if dy + dz + dx == 0:
+                        continue
+                    term = self.into[dy, dz, dx].astype(F32)
+                    total[dy] = term if total[dy] is None else total[dy] + term
+        return total
 
     def finish(self):
         for copy in self.started:
             copy.wait_send()
 
 
-def scatter_shapes(rows):
+def scatter_shapes(rows, wide):
     return [
         pltpu.VMEM((2, 4, 2, 2, rows, 128), BF16),
         pltpu.VMEM((2, 4, 2, rows, 128), BF16),
         pltpu.VMEM((2, 4, 2, rows, 128), BF16),
         pltpu.VMEM((2, 4, rows, 128), BF16),
         pltpu.VMEM((2, 4, rows, 128), BF16),
-        pltpu.VMEM((3, 2, rows, 128), BF16),
-        pltpu.VMEM((2, rows, 128), BF16),
-        pltpu.VMEM((rows, 128), BF16),
-        pltpu.SemaphoreType.DMA((6,)),
-        pltpu.SemaphoreType.DMA((6,)),
+        pltpu.VMEM((2, 4, 2 if wide else 1, rows, 128), BF16),
+        pltpu.SemaphoreType.DMA((17,)),
+        pltpu.SemaphoreType.DMA((17,)),
     ]
 
 
@@ -618,114 +658,194 @@
     def take(count):
         return [next(it) for _ in range(count)]
 
-    attn, fc1, fc2, low_rank, ff_rank, tok, cot, lengths = take(8)
-    layer_out, input_grad, early_out, late_out = take(4)
+    attn, fc1, fc2, tok_far, cot_far, down_table, up_table, ff_table, vec_in, bias_in, lengths, ids = take(12)
+    layer_out, input_grad, down_out, up_out, ff_out = take(5)
     wide, tall, rank_all, ff_all = take(4)
     rank_in, rank_up, rank_x, vec, ff_low, bias = take(6)
     heads_out, heads_in = take(2)
     weights_low, weights_back = take(2)
-    tmp, attended, stat, sum_one, scaled_one, normed, scaled_two, grad_second, grad_first = take(9)
-    mixed, normed_low, out_low, branch_low, query_low, key_low, value_low = take(7)
+    attended, stat, tmp, sum_one, scaled_one, normed, grad_second, grad_first = take(8)
+    tok, cot, mixed, normed_low, out_low, branch_low, query_low, key_low, value_low = take(9)
     slope, act, grad_hidden, inner4 = take(4)
-    early_refs, late_refs = take(10), take(10)
-    own, send, recv, hsend, hrecv = take(5)
+    id_rows, table, rank_other, ff_other = take(4)
+    early_refs, late_refs = take(8), take(8)
+    own, send, recv, hsend, hrecv, id_sem = take(6)
 
     spot = Spot()
     here = (spot.y, spot.z, spot.x, spot.c)
-    parts = [wide.at[k] for k in range(8)] + [tall.at[k] for k in range(4)] + [rank_all, ff_all]
-    sources = [attn.at[j] for j in range(4)]
-    sources += [fc1.at[:, pl.ds(q * 1024, 1024)] for q in range(4)]
-    sources += [fc2.at[:, pl.ds(q * 256, 256)] for q in range(4)] + [low_rank, ff_rank]
-    placed = [pltpu.make_async_copy(sources[k], parts[k].at[here], own.at[k]) for k in ORDER]
-    for copy in placed:
+    parts = [wide.at[k] for k in range(16)] + [tall.at[k] for k in range(8)] + [rank_all, ff_all]
+    placed = {}
+    for k in range(8, 16):
+        placed[k] = fc1.at[:, pl.ds((k - 8) * 512, 512)]
+    for k in range(16, 24):
+        placed[k] = fc2.at[:, pl.ds((k - 16) * 128, 128)]
+    placed = {k: pltpu.make_async_copy(source, parts[k].at[here], own.at[k - 8]) for k, source in placed.items()}
+    tok_copy = pltpu.make_async_copy(tok_far, tok, own.at[16])
+    cot_copy = pltpu.make_async_copy(cot_far, cot, own.at[17])
+    tok_copy.start()
+    for k in (0, 1):
+        wide[(k,) + here] = attn[:, 0, k * 512 : k * 512 + 512]
+    for copy in placed.values():
         copy.start()
-    gather = Gather(spot, [parts[k] for k in ORDER], send, recv)
+    cot_copy.start()
+    others = {2: rank_other, 3: ff_other}
+    gather = Gather(spot, [parts[k] for k in ORDER], WAYS, others, send, recv)
     swaps = Exchange(spot, heads_out, heads_in, hsend, hrecv)
-    early = Scatter(spot, *early_refs)
-    late = Scatter(spot, *late_refs)
+    early = Scatter(spot, False, *early_refs)
+    late = Scatter(spot, True, *late_refs)
+    first_row = lax.broadcasted_iota(jnp.int32, (8, 128), 0) == 0
+    id_rows[spot.y] = jnp.where(first_row, ids[0], ids[1])
     enter(spot)
-    for copy in placed:
-        copy.wait()
+    gather.step(0)
+    id_copy = pltpu.make_async_remote_copy(
+        src_ref=id_rows.at[spot.y],
+        dst_ref=id_rows.at[spot.y],
+        send_sem=id_sem.at[0],
+        recv_sem=id_sem.at[1],
+        device_id=spot.at(dy=1),
+        device_id_type=MESH,
+    )
+    id_copy.start()
+    for j in range(1, 4):
+        for k in range(2):
+            wide[(2 * j + k,) + here] = attn[:, j, k * 512 : k * 512 + 512]
+
+    def chosen(source, kind, y, slot):
+        who = id_rows[y, slot : slot + 1, 0 : source.shape[3]]
+        total = None
+        for a in range(ADAPTERS):
+            term = jnp.where(who == a, source[a, kind].astype(F32), 0.0)
+            total = term if total is None else total + term
+        return total
+
+    def pick_all():
+        table[...] = jnp.zeros_like(table)
+        for g in range(2):
+            y = (spot.y + g) % 2
+            for slot in range(2):
+                for j in range(4):
+                    row = g * 384 + j * 32 + slot * 16
+                    table[row : row + 16, 0:32] = chosen(down_table, j, y, slot)
+                    table[row + 128 : row + 144, 0:32] = chosen(up_table, j, y, slot)
+                row = g * 384 + 256 + slot * 16
+                table[row : row + 16, 0:32] = chosen(down_table, 4, y, slot)
+                table[row + 32 : row + 48, 0:32] = chosen(up_table, 4, y, slot)
+                for kind in range(2):
+                    row = 768 + g * 64 + kind * 32 + slot * 16
+                    table[row : row + 16, :] = chosen(ff_table, kind, y, slot)
+        for n in range(3):
+            cols = slice(n * 128, n * 128 + 128)
+            rank_all[here + (slice(None), cols)] = table[cols, :].T[0:32].astype(BF16)
+            rank_other[:, cols] = table[384 + n * 128 : 512 + n * 128, :].T[0:32].astype(BF16)
+        turned = table[768:896, :].T
+        ff_all[here + (slice(0, 64),)] = pair(turned[0:64], swap(turned[64:128])).astype(BF16)
+        ff_other[0:64] = pair(swap(turned[0:64]), turned[64:128]).astype(BF16)
+        table[0:8, 0:32] = vec_in[...].astype(F32)
+        table[0:8, 32:128] = jnp.zeros((8, 96), F32)
+        columns = pltpu.roll(table[0:8, :], (spot.s % 4) * 32, 1)
+        rows = jnp.concatenate([jnp.broadcast_to(bias_in[...].astype(F32), (8, 128)), columns], axis=0)
+        ff_all[here + (slice(64, 80),)] = rows.astype(BF16)
+        ff_other[64:80] = rows.astype(BF16)
 
     lane = lanes((128, 128))
     row_slot = lax.broadcasted_iota(jnp.int32, (128, 128), 0) >= 64
     slot_lane = ((lane & 16) != 0) == row_slot
     kind4 = [slot_lane & ((lane >> 5) == j) for j in range(4)]
-    kind_ff = [slot_lane & ((lane >> 5) == spot.y * 2 + k) for k in range(2)]
+    kind_ff = [slot_lane & ((lane >> 5) == k) for k in range(2)]
 
     def only(mask, value):
         return jnp.where(mask, value, jnp.zeros_like(value))
 
     def square(k, t):
-        return wide[k, t // 2, pl.ds((t % 2) * 2, 2)].reshape(256, 1024)
-
-    def columns(k, cols):
-        return wide[k, :, :, :, :, :, cols].reshape(1024, 256)
+        halves = [wide[2 * k + i, t // 2, pl.ds((t % 2) * 2, 2)].reshape(256, 512) for i in range(2)]
+        return jnp.concatenate(halves, axis=1)
+
+    def columns(k, n):
+        return wide[2 * k + n // 2, :, :, :, :, :, tile(n % 2)].reshape(1024, 256)
 
     def tile(n, size=256):
         return pl.ds(pl.multiple_of(n * size, size), size)
 
     def unpack_rank():
-        y_lanes = pl.ds(pl.multiple_of(spot.y * 128, 128), 128)
-        up_lanes = pl.ds(pl.multiple_of(spot.y * 128 + 256, 128), 128)
-        rank_in[...] = rank_all[:, :, :, :, :, y_lanes].reshape(1024, 128)
-        rank_up[...] = rank_all[:, :, :, :, :, up_lanes].reshape(1024, 128)
-        rank_x[...] = rank_all[:, :, :, :, :, 512:640].reshape(1024, 128)
-        vec[...] = rank_all[:, :, :, :, :, 640:768].reshape(1024, 128).astype(F32).T[0:8]
+        rank_in[...] = rank_all[:, :, :, :, :, 0:128].reshape(1024, 128)
+        rank_up[...] = rank_all[:, :, :, :, :, 128:256].reshape(1024, 128)
+        rank_x[...] = rank_all[:, :, :, :, :, 256:384].reshape(1024, 128)
+
+    def ff_rows(first, count):
+        return ff_low[pl.ds(first, count)].reshape(count * 128, 128)
 
     def unpack_ff():
-        ff_low[...] = ff_all[:, :, :, :, 0:128, :].reshape(4096, 128)
+        columns_of = {}
+        packed = ff_all[:, :, :, :, 0:64, :].reshape(32, 64, 128)
+        ff_low[:, 0] = packed
+        ff_low[:, 1] = swap(packed.astype(F32).reshape(2048, 128)).astype(BF16).reshape(32, 64, 128)
         for o in range(32):
             y, z, x, c = o // 16, (o // 4) % 4, (o // 2) % 2, o % 2
-            bias[:, o * 128 : o * 128 + 128] = ff_all[y, z, x, c, 128:136, :].astype(F32)
+            rows = ff_all[y, z, x, c, 64:80, :].astype(F32)
+            bias[:, o * 128 : o * 128 + 128] = rows[0:8]
+            columns_of[o // 4] = rows[8:16] if o % 4 == 0 else columns_of[o // 4] + rows[8:16]
+        for n in range(8):
+            vec[:, n * 128 : n * 128 + 128] = columns_of[n]
+
+    def to_heads(unit, block, value):
+        for p in range(2):
+            first = value[0:64, p * 128 : p * 128 + 128]
+            second = value[64:128, p * 128 : p * 128 + 128]
+            heads_out[unit, block * 4 + 2 * p] = pair(first, swap(second)).astype(BF16)
+            heads_out[unit, block * 4 + 2 * p + 1] = pair(swap(first), second).astype(BF16)
+        swaps.start(unit, block)
+
+    def turn(body):
+        def shifted(t, carry):
+            body((spot.z + t) % 4)
+            return carry
+
+        lax.fori_loop(0, 4, shifted, 0)
 
     def project_in(j):
         inner = only(kind4[j], inner4[...])
 
-        def body(n, carry):
+        def body(n):
             cols = tile(n)
-            value = dot(tok[...], columns(j, cols)) + dot_nt(inner, rank_up[cols, :])
+            value = dot(tok[...], columns(j, n)) + dot_nt(inner, rank_up[cols, :])
             if j == 0:
                 value = (value + vec[0:1, cols]) * 0.125
             if j == 2:
                 value = value + vec[1:2, cols]
-            tmp[:, cols] = value
-            return carry
-
-        lax.fori_loop(0, 4, body, 0)
-        rows_to_heads(tmp, heads_out.at[j])
-        swaps.start(j)
-
-    def attention():
-        for j in range(3):
-            swaps.wait(j)
+            to_heads(j, n, value)
+
+        turn(body)
+        swaps.keep(j)
+
+    def attention(t):
+        if t == 0:
+            for j in range(3):
+                swaps.wait(j)
+        block = (spot.z + t) % 4
         keys = heads_in[1].reshape(1024, 128)
         values = heads_in[2].reshape(1024, 128)
-
-        def body(t, carry):
-            rows = tile(t)
-            query = heads_in[0, pl.ds(t * 4, 4)].reshape(256, 128)
-            results, stats = [], []
-            for slot in range(2):
-                scores = dot_nt(half(query, slot), keys)
-                scores = jnp.where(lanes(scores.shape) < lengths[slot], scores, NEG_FILL)
-                top = jnp.max(scores, axis=-1, keepdims=True)
-                shifted = jnp.exp(scores - top)
-                total = jnp.sum(shifted, axis=-1, keepdims=True)
-                low = (shifted * (1.0 / total)).astype(BF16)
-                weights_low[slot, rows, :] = low
-                results.append(dot(low, values))
-                stats.append(jnp.broadcast_to(top + jnp.log(total), (256, 128)))
-            result = pair(results[0], results[1])
-            attended[rows, :] = result
-            heads_out[3, pl.ds(t * 4, 4)] = result.astype(BF16).reshape(4, 64, 128)
-            stat[rows, :] = pair(stats[0], stats[1])
-            return carry
-
-        lax.fori_loop(0, 4, body, 0)
-        swaps.start(3)
-
-    def attention_turned():
+        rows = tile(block)
+        query = heads_in[0, pl.ds(block * 4, 4)].reshape(256, 128)
+        results, stats = [], []
+        for slot in range(2):
+            scores = dot_nt(half(query, slot), keys)
+            scores = jnp.where(lanes(scores.shape) < lengths[slot], scores, NEG_FILL)
+            top = jnp.max(scores, axis=-1, keepdims=True)
+            shifted = jnp.exp(scores - top)
+            total = jnp.sum(shifted, axis=-1, keepdims=True)
+            low = (shifted * (1.0 / total)).astype(BF16)
+            weights_low[slot, rows, :] = low
+            results.append(dot(low, values))
+            stats.append(jnp.broadcast_to(top + jnp.log(total), (256, 128)))
+        result = pair(results[0], results[1])
+        attended[rows, :] = result
+        heads_out[3, pl.ds(block * 4, 4)] = result.astype(BF16).reshape(4, 64, 128)
+        stat[rows, :] = pair(stats[0], stats[1])
+        swaps.start(3, block)
+        if t == 3:
+            swaps.keep(3)
+
+    def attention_turned(first):
         logsum = stat[...].T
         queries = heads_in[0].reshape(1024, 128)
         turned = [logsum[0:1], logsum[64:65]]
@@ -741,7 +861,7 @@
                 weights_back[slot, rows, :] = weights.astype(BF16)
             return carry
 
-        lax.fori_loop(0, 4, body, 0)
+        lax.fori_loop(first, first + 2, body, 0)
 
     def normalize(value):
         centered = value - jnp.mean(value, axis=-1, keepdims=True)
@@ -762,7 +882,7 @@
 
         def body(n, carry):
             cols = tile(n)
-            value = dot(mixed[...], columns(3, cols)) + dot_nt(saved["o"], rank_up[cols, :])
+            value = dot(mixed[...], columns(3, n)) + dot_nt(saved["o"], rank_up[cols, :])
             sum_one[:, cols] = tok[:, cols].astype(F32) + value + vec[2:3, cols]
             return carry
 
@@ -774,25 +894,26 @@
         normed_low[...] = value.astype(BF16)
         saved["hidden"] = only(kind_ff[0], dot(normed_low[...], rank_x[...])).astype(BF16)
 
-    def expand(q):
-        def body(n, carry):
+    def expand(k):
+        def body(i, carry):
+            n = k * 2 + i
             cols = tile(n)
-            wide_cols = tile(q * 4 + n)
-            value = dot(normed_low[...], columns(4 + q, cols))
-            value = value + dot_nt(saved["hidden"], ff_low[wide_cols, :]) + bias[0:1, wide_cols]
+            value = dot(normed_low[...], wide[8 + k, :, :, :, :, :, tile(i)].reshape(1024, 256))
+            value = value + dot_nt(saved["hidden"], ff_rows(n * 2, 2)) + bias[0:1, cols]
             share = 0.5 * (1.0 + lax.erf(value * math.sqrt(0.5)))
-            act[:, wide_cols] = (value * share).astype(BF16)
+            act[:, cols] = (value * share).astype(BF16)
             bell = jnp.exp(-0.5 * value * value) * (1.0 / math.sqrt(2.0 * math.pi))
-            slope[:, wide_cols] = share + value * bell
+            slope[:, cols] = share + value * bell
             return carry
 
-        lax.fori_loop(0, 4, body, 0)
+        lax.fori_loop(0, 2, body, 0)
 
     def contract(q):
         if q == 0:
-            saved["out"] = only(kind_ff[1], dot(act[...], ff_low[...])).astype(BF16)
-        cols = pl.ds(q * 256, 256)
-        value = dot(act[...], tall[q].reshape(4096, 256)) + dot_nt(saved["out"], rank_x[cols, :])
+            saved["out"] = only(kind_ff[1], dot(act[...], ff_rows(0, 32))).astype(BF16)
+        cols = slice(q * 256, q * 256 + 256)
+        weight = jnp.concatenate([tall[2 * q + i].reshape(4096, 128) for i in range(2)], axis=1)
+        value = dot(act[...], weight) + dot_nt(saved["out"], rank_x[cols, :])
         tmp[:, cols] = normed[:, cols] + value + vec[3:4, cols]
 
     def outer():
@@ -810,15 +931,16 @@
     def hidden_back():
         def body(t, carry):
             rows = tile(t, 512)
-            value = dot_nt(saved["g_out"], ff_low[rows, :])
+            value = dot_nt(saved["g_out"], ff_rows(t * 4, 4))
             for q in range(4):
-                piece = tall[q, t // 4, t % 4].reshape(512, 256)
+                pieces = [tall[2 * q + i, t // 4, t % 4].reshape(512, 128) for i in range(2)]
+                piece = jnp.concatenate(pieces, axis=1)
                 value = value + dot_nt(out_low[:, q * 256 : q * 256 + 256], piece)
             grad_hidden[:, rows] = (value * slope[:, rows]).astype(BF16)
             return carry
 
         lax.fori_loop(0, 8, body, 0)
-        saved["g_hidden"] = only(kind_ff[0], dot(grad_hidden[...], ff_low[...])).astype(BF16)
+        saved["g_hidden"] = only(kind_ff[0], dot(grad_hidden[...], ff_rows(0, 32))).astype(BF16)
 
     def normed_back():
         def body(t, carry):
@@ -836,19 +958,19 @@
         saved["g_o"] = only(kind4[3], dot(branch_low[...], rank_up[...])).astype(BF16)
 
     def mixed_back():
-        def body(t, carry):
-            rows = tile(t)
-            tmp[:, rows] = dot_nt(branch_low[...], square(3, t)) + dot_nt(saved["g_o"], rank_in[rows, :])
-            return carry
-
-        lax.fori_loop(0, 4, body, 0)
-        rows_to_heads(tmp, heads_out.at[4])
-        swaps.start(4)
+        def body(n):
+            value = dot_nt(branch_low[...], square(3, n)) + dot_nt(saved["g_o"], rank_in[tile(n), :])
+            to_heads(4, n, value)
+
+        turn(body)
+        swaps.keep(4)
 
     def early_grads():
         own_grads = early.own
         value = dot_tn(normed_low[...], saved["g_hidden"]) + dot_tn(out_low[...], saved["out"])
-        own_grads[:, :, :, :, 0:32, :] = value.astype(BF16).reshape(2, 4, 2, 2, 32, 128)
+        value = value.reshape(32, 2, 16, 128)
+        value = value[:, 0] + swap(value[:, 1].reshape(512, 128)).reshape(32, 16, 128)
+        own_grads[:, :, :, :, 0:16, :] = value.astype(BF16).reshape(2, 4, 2, 2, 16, 128)
         for y in range(2):
             for z in range(4):
                 cols = slice((y * 4 + z) * 512, (y * 4 + z) * 512 + 512)
@@ -856,23 +978,39 @@
                 value = value.reshape(4, 128, 128)
                 for o in range(4):
                     packed = value[o, 0:64] + swap(value[o, 64:128])
-                    own_grads[y, z, o // 2, o % 2, 32:96, :] = packed.astype(BF16)
-
-    def attention_back():
-        swaps.wait(4)
+                    own_grads[y, z, o // 2, o % 2, 16:80, :] = packed.astype(BF16)
+
+    def query_back(t):
+        block = (spot.z + 4 - t) % 4
+        swaps.wait_block(4, block)
+        rows = tile(block)
         keys = heads_in[1].reshape(1024, 128)
         values = heads_in[2].reshape(1024, 128)
+        grad_block = heads_in[4, pl.ds(block * 4, 4)].reshape(256, 128)
+        product = grad_block.astype(F32) * attended[rows, :]
+        parts_, deltas = [], []
+        for slot in range(2):
+            delta = jnp.sum(half(product, slot), axis=-1, keepdims=True)
+            grad_probs = dot_nt(half(grad_block, slot), values)
+            weights = weights_low[slot, rows, :].astype(F32)
+            grad_scores = (weights * (grad_probs - delta)).astype(BF16)
+            parts_.append(dot(grad_scores, keys))
+            deltas.append(jnp.broadcast_to(delta, (256, 128)))
+        heads_out[5, pl.ds(block * 4, 4)] = pair(*parts_).astype(BF16).reshape(4, 64, 128)
+        stat[rows, :] = pair(*deltas)
+        swaps.start(5, block)
+        if t == 3:
+            swaps.keep(5)
+
+    def key_back():
         queries = heads_in[0].reshape(1024, 128)
         grads = heads_in[4].reshape(1024, 128)
-        product = grads.astype(F32) * attended[...]
-        deltas = [jnp.sum(half(product, slot), axis=-1, keepdims=True) for slot in range(2)]
-        stat[...] = pair(*[jnp.broadcast_to(delta, (1024, 128)) for delta in deltas])
         turned = stat[...].T
         turned = [turned[0:1], turned[64:65]]
 
-        def key_side(t, carry):
-            rows = tile(t)
-            value_block = heads_in[2, pl.ds(t * 4, 4)].reshape(256, 128)
+        def body(block):
+            rows = tile(block)
+            value_block = heads_in[2, pl.ds(block * 4, 4)].reshape(256, 128)
             key_parts, value_parts = [], []
             for slot in range(2):
                 weights = weights_back[slot, rows, :]
@@ -880,38 +1018,22 @@
                 grad_scores = (weights.astype(F32) * (grad_probs - turned[slot])).astype(BF16)
                 key_parts.append(dot(grad_scores, queries))
                 value_parts.append(dot(weights, grads))
-            heads_out[6, pl.ds(t * 4, 4)] = pair(*key_parts).astype(BF16).reshape(4, 64, 128)
-            heads_out[7, pl.ds(t * 4, 4)] = pair(*value_parts).astype(BF16).reshape(4, 64, 128)
-            return carry
-
-        lax.fori_loop(0, 4, key_side, 0)
-        swaps.start(6)
-        swaps.start(7)
-
-        def query_side_block(t, carry):
-            rows = tile(t)
-            grad_block = heads_in[4, pl.ds(t * 4, 4)].reshape(256, 128)
-            delta_block = stat[rows, :]
-            query_parts = []
-            for slot in range(2):
-                grad_probs = dot_nt(half(grad_block, slot), values)
-                delta = delta_block[:, 64 * slot : 64 * slot + 1]
-                weights = weights_low[slot, rows, :].astype(F32)
-                grad_scores = (weights * (grad_probs - delta)).astype(BF16)
-                query_parts.append(dot(grad_scores, keys))
-            heads_out[5, pl.ds(t * 4, 4)] = pair(*query_parts).astype(BF16).reshape(4, 64, 128)
-            return carry
-
-        lax.fori_loop(0, 4, query_side_block, 0)
-        swaps.start(5)
+            heads_out[6, pl.ds(block * 4, 4)] = pair(*key_parts).astype(BF16).reshape(4, 64, 128)
+            heads_out[7, pl.ds(block * 4, 4)] = pair(*value_parts).astype(BF16).reshape(4, 64, 128)
+            swaps.start(6, block)
+            swaps.start(7, block)
+
+        turn(body)
+        swaps.keep(6)
+        swaps.keep(7)
 
     def inputs_back():
+        swaps.wait(5)
+        heads_to_rows(heads_in.at[5], query_low, 0.125)
         swaps.wait(6)
         heads_to_rows(heads_in.at[6], key_low, 1.0)
         swaps.wait(7)
         heads_to_rows(heads_in.at[7], value_low, 1.0)
-        swaps.wait(5)
-        heads_to_rows(heads_in.at[5], query_low, 0.125)
         grads = (query_low, key_low, value_low)
         inner = jnp.zeros((128, 128), F32)
         for j in range(3):
@@ -931,54 +1053,117 @@
             value = value + dot_nt(grad[...], square(j, t))
         input_grad[:, rows] = value.astype(BF16)
 
-    for t in range(CHUNKS + 4):
+    def results(early_sum, late_sum):
+        turned, ff_turned = [], []
+        for dy in range(2):
+            cross = jnp.concatenate([early_sum[dy][0:16], swap(early_sum[dy][0:16])], axis=0)
+            table[0:64, :] = late_sum[dy]
+            table[64:96, :] = cross
+            table[96:128, :] = jnp.zeros((32, 128), F32)
+            turned.append(table[0:128, :].T)
+            packed = early_sum[dy][16:80]
+            ff_turned.append(jnp.concatenate([packed, swap(packed)], axis=0).T)
+        for a in range(ADAPTERS):
+            who = [id_rows[(spot.y + dy) % 2, 0:2, :] == a for dy in range(2)]
+            share = [match.astype(F32) for match in who]
+
+            def gathered(source, first):
+                total = None
+                for dy in range(2):
+                    for s in range(2):
+                        row = first + s * 16
+                        term = share[dy][s : s + 1] * source[dy][row : row + 16, :]
+                        total = term if total is None else total + term
+                return total
+
+            for j in range(4):
+                value = gathered(turned, j * 32)
+                down_out[a, j] = value[:, 0:32]
+                up_out[a, j] = value[:, 32:64]
+            down_out[a, 4] = gathered(turned, 0)[:, 64:96]
+            up_out[a, 4] = gathered(turned, 32)[:, 64:96]
+            for kind in range(2):
+                ff_out[a, kind] = gathered(ff_turned, kind * 32)
+
+    waited = set()
+
+    def here_by(last):
+        for k in ORDER[: last + 1]:
+            if k in placed and k not in waited:
+                placed[k].wait()
+                waited.add(k)
+
+    for t in range(1, CHUNKS + 4):
+        if t == 2:
+            id_copy.wait_recv()
+            pick_all()
+        here_by(min(t, CHUNKS - 1))
         gather.step(t)
-        if t == 5:
+        if t == 7:
+            tok_copy.wait()
             unpack_rank()
+            unpack_ff()
             inner4[...] = dot(tok[...], rank_in[...]).astype(BF16)
-        if 5 <= t <= 7:
-            project_in(t - 5)
-        if t == 9:
-            unpack_ff()
-            attention()
-        if t == 10:
-            attention_turned()
-        if t == 11:
+        if t in (7, 9, 11):
+            project_in((t - 7) // 2)
+        if 14 <= t <= 17:
+            attention(t - 14)
+        if 18 <= t <= 19:
+            attention_turned((t - 18) * 2)
+        if t == 20:
             branch()
-            expand(0)
-            expand(1)
-        if 12 <= t <= 13:
-            expand(t - 10)
-        if t >= 14:
-            contract(t - 14)
+        if 21 <= t <= 24:
+            expand(2 * t - 42)
+            expand(2 * t - 41)
+        if t == 27:
+            contract(0)
+        if t >= 27:
+            contract(t - 26)
+    cot_copy.wait()
     outer()
     hidden_back()
     normed_back()
     mixed_back()
     early_grads()
     early.first()
+    for t in range(4):
+        query_back(t)
     early.second()
-    attention_back()
+    key_back()
     early.third()
-    early.fourth(early_out)
     inputs_back()
     late.first()
     tokens_back(0)
     late.second()
-    tokens_back(1)
-    tokens_back(2)
     late.third()
-    tokens_back(3)
-    late.fourth(late_out)
-    early.fifth(early_out)
-    late.fifth(late_out)
+    for t in range(1, 4):
+        tokens_back(t)
+    results(early.fourth(), late.fourth())
+    id_copy.wait_send()
     gather.finish()
     swaps.finish(8)
     early.finish()
     late.finish()
 
 
-def layer(attn, fc1, fc2, low_rank, ff_rank, tok, cot, lengths):
+def hand_on_kernel(*refs):
+    count = len(refs) // 2
+    for k in range(count):
+        refs[count + k][...] = refs[k][...]
+
+
+def hand_on(arrays):
+    near = pl.BlockSpec(memory_space=pltpu.VMEM)
+    return pl.pallas_call(
+        hand_on_kernel,
+        out_shape=[jax.ShapeDtypeStruct(array.shape, array.dtype) for array in arrays],
+        in_specs=[near] * len(arrays),
+        out_specs=[near] * len(arrays),
+        name="hand_on",
+    )(*arrays)
+
+
+def layer(attn, fc1, fc2, tok, cot, down, up, ff, vec, bias, lengths, ids):
     lead = (2, 4, 2, 2)
     anywhere = pl.BlockSpec(memory_space=pl.ANY)
     near = pl.BlockSpec(memory_space=pltpu.VMEM)
@@ -988,39 +1173,43 @@
         return pltpu.VMEM(shape, dtype)
 
     scratch = [
-        buffer(8, *lead, 32, 1024),
-        buffer(4, *lead, 128, 256),
-        buffer(*lead, *low_rank.shape),
-        buffer(*lead, *ff_rank.shape),
+        buffer(16, *lead, 32, 512),
+        buffer(8, *lead, 128, 128),
+        buffer(*lead, 32, 384),
+        buffer(*lead, 80, 128),
     ]
-    scratch += [buffer(1024, 128)] * 3 + [buffer(8, 1024, dtype=F32), buffer(4096, 128)]
+    scratch += [buffer(1024, 128)] * 3 + [buffer(8, 1024, dtype=F32), buffer(32, 2, 64, 128)]
     scratch += [buffer(8, 4096, dtype=F32)]
     scratch += [buffer(8, 16, 64, 128)] * 2
     scratch += [buffer(2, 1024, 1024)] * 2
-    scratch += [buffer(128, 1024, dtype=F32)] + [buffer(1024, 128, dtype=F32)] * 2
+    scratch += [buffer(1024, 128, dtype=F32)] * 2
     scratch += [buffer(128, 1024, dtype=F32)] * 6
-    scratch += [buffer(128, 1024)] * 7
+    scratch += [buffer(128, 1024)] * 9
     scratch += [buffer(128, 4096, dtype=F32), buffer(128, 4096), buffer(128, 4096), buffer(128, 128)]
-    scratch += scatter_shapes(EARLY) + scatter_shapes(LATE)
-    scratch += [pltpu.SemaphoreType.DMA((CHUNKS,))]
+    scratch += [buffer(2, 8, 128, dtype=jnp.int32), buffer(896, 128, dtype=F32)]
+    scratch += [buffer(32, 384), buffer(80, 128)]
+    scratch += scatter_shapes(EARLY, False) + scatter_shapes(LATE, True)
+    scratch += [pltpu.SemaphoreType.DMA((18,))]
     scratch += [pltpu.SemaphoreType.DMA((CHUNKS, ROUTES))] * 2
     scratch += [pltpu.SemaphoreType.DMA((8, 16))] * 2
+    scratch += [pltpu.SemaphoreType.DMA((2,))]
     return pl.pallas_call(
         layer_kernel,
         out_shape=[
             jax.ShapeDtypeStruct(tok.shape, BF16),
             jax.ShapeDtypeStruct(tok.shape, BF16),
-            jax.ShapeDtypeStruct((2, EARLY, 128), F32),
-            jax.ShapeDtypeStruct((2, LATE, 128), F32),
+            jax.ShapeDtypeStruct(down.shape, F32),
+            jax.ShapeDtypeStruct(up.shape, F32),
+            jax.ShapeDtypeStruct(ff.shape, F32),
         ],
-        in_specs=[anywhere] * 5 + [near] * 2 + [scalar],
-        out_specs=[near] * 4,
+        in_specs=[near] + [anywhere] * 4 + [near] * 5 + [scalar] * 2,
+        out_specs=[near] * 5,
         scratch_shapes=scratch,
         compiler_params=pltpu.CompilerParams(
             collective_id=0, has_side_effects=True, vmem_limit_bytes=63 * 2**20
         ),
         name="layer",
-    )(attn, fc1, fc2, low_rank, ff_rank, tok, cot, lengths)
+    )(attn, fc1, fc2, tok, cot, down, up, ff, vec, bias, lengths, ids)
 
 
 def fast_device(
@@ -1037,58 +1226,24 @@
     adapter_up,
     ff_adapters,
 ):
-    rows, width = adapter_down.shape[0], tokens.shape[2]
-    ff_rows = ff_adapters.shape[0]
-    ids = lax.all_gather(adapter_ids, "fsdp", axis=0, tiled=True)
-    onehot = ids[:, None] == jnp.arange(ADAPTERS)[None, :]
-
-    def pick(table):
-        picked = jnp.einsum("si,dikr->dskr", onehot.astype(BF16), table, preferred_element_type=F32)
-        picked = picked.astype(BF16).reshape(table.shape[0], 2, 2, table.shape[2], 16)
-        return picked.transpose(0, 1, 3, 2, 4)
-
-    down, up, ff_part = pick(adapter_down), pick(adapter_up), pick(ff_adapters)
-    cross = jnp.stack([down[:, :, 4], up[:, :, 4]], axis=2)
-    low_rank = jnp.concatenate(
-        [
-            down[:, :, :4].reshape(rows, 256),
-            up[:, :, :4].reshape(rows, 256),
-            cross.reshape(rows, 128),
-            jnp.pad(vectors, ((0, 0), (0, 120))),
-        ],
-        axis=1,
-    )
-    bias_rows = jnp.broadcast_to(fc1_bias[None], (16, ff_rows))
-    ff_rank = jnp.concatenate([ff_part.reshape(ff_rows, 128), bias_rows], axis=0)
-    layer_out, input_grad, early, late = layer(
-        attn_weight.transpose(1, 0, 2),
+    width = tokens.shape[2]
+    outs = layer(
+        attn_weight,
         fc1_weight,
         fc2_weight,
-        low_rank,
-        ff_rank,
         tokens.reshape(-1, width),
         cotangent.reshape(-1, width),
+        adapter_down.transpose(1, 2, 3, 0),
+        adapter_up.transpose(1, 2, 3, 0),
+        ff_adapters.transpose(1, 2, 3, 0),
+        vectors.T,
+        fc1_bias[None],
         lengths,
-    )
-    picks = onehot.astype(F32).reshape(2, 2, ADAPTERS)
-    four = late.reshape(2, 2, rows, 4, 2, 16)
-    cross = early[:, :rows].reshape(2, rows, 2, 64)
-    cross = jnp.stack([cross[0, :, 0], cross[1, :, 1]]).reshape(2, rows, 2, 2, 16)
-    packed = early[:, rows:]
-    ff_first = jnp.concatenate([packed[0, :, :64], packed[0, :, 64:]], axis=0)
-    ff_second = jnp.concatenate([packed[1, :, 64:], packed[1, :, :64]], axis=0)
-    ff_terms = jnp.stack([ff_first, ff_second]).reshape(2, ff_rows, 2, 2, 16)
-
-    def spread(terms):
-        return jnp.einsum("ysi,ydksr->dikr", picks, terms, precision=lax.Precision.HIGHEST)
-
-    return (
-        layer_out.reshape(tokens.shape),
-        input_grad.reshape(tokens.shape),
-        spread(jnp.concatenate([four[:, 0], cross[:, :, 0:1]], axis=2)),
-        spread(jnp.concatenate([four[:, 1], cross[:, :, 1:2]], axis=2)),
-        spread(ff_terms),
-    )
+        adapter_ids,
+    )
+    outs = hand_on(outs)
+    grads = [grad.transpose(3, 0, 1, 2) for grad in outs[2:]]
+    return (outs[0].reshape(tokens.shape), outs[1].reshape(tokens.shape), *grads)
 
 
 def solution(mesh):

time: 235 us -> 205 us (0.87)
  local copies, waits for them, and re-layouts: 12.5 us -> 0 us
  Pallas kernels: 212 us -> 205 us
  blocking collectives: 5.22 us -> 0 us
    unnamed x32 -> x0, local copies, waits for them, and re-layouts: 9.72 us -> none
    pallas_call x1, Pallas kernels: 212 us -> 202 us  [layer(): pl.pallas_call(layer_kernel, out_shape=[jax.ShapeDtypeStruct(tok.shape, B...]
    unnamed x1 -> x0, blocking collectives: 5.22 us -> none
where the time goes in v2:
time: 205 us
  Pallas kernels  205 us (100%)
    pallas_call x1, Pallas kernels, layer(): pl.pallas_call(layer_kernel, out_shape=[jax.ShapeDtypeStruct(tok.shape, B...  202 us

profile of v2, /device:TPU:0, one launch (start us, length us, event | category | flops | bytes accessed | tf_op | source)
XLA Modules:
  0.0 205.3 jit_solution(7391086011352098841)
XLA Ops:
  0.6 202.3 %layer.1 = (bf16[128,1024]{1,0:T(8,128)(2,1)}, bf16[128,1024]{1,0:T(8,128)(2,1)}, f32[8,5,16,32]{3,2,1,0:T(8,128)}, f32[8,5,16,32]{3,2,1,0:T(8,128)}, f32[8,2,16,128]{3,2,1,0:T(8,128)}) custom-call(bf16[32,4,1024]{2,1,0:T(4,128)(2,1)} %refs_0_.1, bf16[32,4096]{1,0:T(8,128)(2,1)} %refs_1_.1, bf16[128,1024]{1,0:T(8,128)(2,1)} %refs_2_.1, ...), custom_call_target="tpu_custom_call" | custom-call | tf_op jit(solution)/shard_map/layer/pallas_call | solution.py:1196
  203.0 2.3 %hand_on.1 = (bf16[128,1024]{1,0:T(8,128)(2,1)}, bf16[128,1024]{1,0:T(8,128)(2,1)}, f32[8,5,16,32]{3,2,1,0:T(8,128)}, f32[8,5,16,32]{3,2,1,0:T(8,128)}, f32[8,2,16,128]{3,2,1,0:T(8,128)}) custom-call(bf16[128,1024]{1,0:T(8,128)(2,1)} %get-tuple-element.15.refs_0_, bf16[128,1024]{1,0:T(8,128)(2,1)} %get-tuple-element.16.refs_1_, ...), custom_call_target="tpu_custom_call" | custom-call | tf_op jit(solution)/shard_map/hand_on/pallas_call | solution.py:1157

commit v3 on v2

--- a/solution.py
+++ b/solution.py
@@ -339,7 +339,7 @@
 
 MESH = pl.DeviceIdType.MESH
 CHUNKS = 26
-ROUTES = 11
+DEPTH = 8
 ALL2, ALL4 = pl.ds(0, 2), pl.ds(0, 4)
 
 
@@ -372,86 +372,84 @@
     def __init__(self, spot, parts, ways, others, send, recv):
         self.spot, self.parts, self.ways, self.others = spot, parts, ways, others
         self.send, self.recv = send, recv
-        self.started = []
 
     def block(self, k, dy=0, dz=0, dx=0, dc=0):
         p = self.spot
         places = ((p.y, dy, 2), (p.z, dz, 4), (p.x, dx, 2), (p.c, dc, 2))
         return self.parts[k].at[tuple((place + d) % n if isinstance(d, int) else d for place, d, n in places)]
 
-    def copy(self, source, target, k, route, peer):
+    def copy(self, source, target, k, out, into, peer):
         return pltpu.make_async_remote_copy(
             src_ref=source,
             dst_ref=target,
-            send_sem=self.send.at[k, route],
-            recv_sem=self.recv.at[k, route],
+            send_sem=self.send.at[k % DEPTH, out],
+            recv_sem=self.recv.at[k % DEPTH, into],
             device_id=peer,
             device_id_type=MESH,
         )
 
-    def push(self, ref, k, route, source=None, **hop):
-        copy = self.copy(ref if source is None else source, ref, k, route, self.spot.at(**hop))
-        copy.start()
-        self.started.append(copy)
-
-    def arrive(self, ref, k, route):
-        self.copy(ref, ref, k, route, self.spot.at(dc=1)).wait_recv()
+    def push(self, ref, k, out, into, source=None, **hop):
+        self.copy(ref if source is None else source, ref, k, out, into, self.spot.at(**hop)).start()
+
+    def arrive(self, like, k, into):
+        self.copy(like, like, k, 0, into, self.spot.at(dc=1)).wait_recv()
+
+    def retire(self, k):
+        if self.ways[k] == "z":
+            pieces = ((1, 3, 1), (2, 3, 2), (2, 3, 2), (1, 4, 1))
+        else:
+            pieces = ((1, 1, 1), (2, 3, 1), (2, 4, 2), (2, 4, 1))
+        for out, (ys, zs, xs) in enumerate(pieces):
+            like = self.parts[k].at[pl.ds(0, ys), pl.ds(0, zs), pl.ds(0, xs), 0]
+            self.copy(like, like, k, out, 0, self.spot.at(dc=1)).wait_send()
 
     def first(self, k):
+        if k >= DEPTH:
+            self.retire(k - DEPTH)
         if self.ways[k] == "z":
             for d in range(1, 4):
-                self.push(self.block(k), k, d - 1, dz=d)
+                self.push(self.block(k), k, 0, 0, dz=d)
         else:
-            self.push(self.block(k), k, 0, self.others.get(k), **{"d" + self.ways[k]: 1})
+            self.push(self.block(k), k, 0, 0, self.others.get(k), **{"d" + self.ways[k]: 1})
 
     def second(self, k):
         if self.ways[k] == "z":
+            self.arrive(self.block(k, dz=pl.ds(0, 3)), k, 0)
+            line = self.block(k, dz=ALL4)
+            self.push(line, k, 1, 1, dx=1)
+            self.push(line, k, 1, 2, dy=1)
+            self.push(line, k, 1, 4, dc=1)
+        else:
+            self.arrive(self.block(k), k, 0)
             for d in range(1, 4):
-                self.arrive(self.block(k, dz=4 - d), k, d - 1)
-            line = self.block(k, dz=ALL4)
-            self.push(line, k, 3, dx=1)
-            self.push(line, k, 4, dy=1)
-            self.push(line, k, 5, dc=1)
-        else:
-            self.arrive(self.block(k, **{"d" + self.ways[k]: 1}), k, 0)
-            for d in range(1, 4):
-                self.push(self.block(k, **{"d" + self.ways[k]: ALL2}), k, d, dz=d)
+                self.push(self.block(k, **{"d" + self.ways[k]: ALL2}), k, 1, 1, dz=d)
 
     def third(self, k):
         if self.ways[k] == "z":
-            self.arrive(self.block(k, dz=ALL4, dx=1), k, 3)
-            self.push(self.block(k, dz=pl.ds(0, 2), dx=1), k, 6, dy=1)
-            self.arrive(self.block(k, dz=ALL4, dy=1), k, 4)
-            self.push(self.block(k, dz=pl.ds(2, 2), dy=1), k, 7, dx=1)
-            self.push(self.block(k, dz=ALL4, dx=1), k, 8, dc=1)
-            self.push(self.block(k, dz=ALL4, dy=1), k, 9, dc=1)
+            self.arrive(self.block(k, dz=ALL4), k, 1)
+            self.push(self.block(k, dz=pl.ds(0, 2), dx=1), k, 2, 3, dy=1)
+            self.arrive(self.block(k, dz=ALL4), k, 2)
+            self.push(self.block(k, dz=pl.ds(2, 2), dy=1), k, 2, 3, dx=1)
+            self.push(self.block(k, dz=ALL4, dx=1), k, 2, 4, dc=1)
+            self.push(self.block(k, dz=ALL4, dy=1), k, 2, 4, dc=1)
         else:
             near, far = "d" + self.ways[k], "dy" if self.ways[k] == "x" else "dx"
-            for d in range(1, 4):
-                self.arrive(self.block(k, **{near: ALL2, "dz": 4 - d}), k, d)
+            self.arrive(self.block(k, **{near: ALL2, "dz": pl.ds(0, 3)}), k, 1)
             plane = self.block(k, **{near: ALL2, "dz": ALL4})
-            self.push(plane, k, 4, **{far: 1})
-            self.push(plane, k, 5, dc=1)
+            self.push(plane, k, 2, 2, **{far: 1})
+            self.push(plane, k, 2, 4, dc=1)
 
     def fourth(self, k):
         if self.ways[k] == "z":
-            self.arrive(self.block(k, dz=pl.ds(0, 2), dx=1, dy=1), k, 6)
-            self.arrive(self.block(k, dz=pl.ds(2, 2), dx=1, dy=1), k, 7)
-            self.push(self.block(k, dz=ALL4, dx=1, dy=1), k, 10, dc=1)
+            self.arrive(self.block(k, dz=ALL4), k, 3)
+            self.push(self.block(k, dz=ALL4, dx=1, dy=1), k, 3, 4, dc=1)
         else:
             near, far = "d" + self.ways[k], "dy" if self.ways[k] == "x" else "dx"
-            plane = self.block(k, **{near: ALL2, "dz": ALL4, far: 1})
-            self.arrive(plane, k, 4)
-            self.push(plane, k, 6, dc=1)
+            self.arrive(self.block(k, **{near: ALL2, "dz": ALL4}), k, 2)
+            self.push(self.block(k, **{near: ALL2, "dz": ALL4, far: 1}), k, 3, 4, dc=1)
 
     def ready(self, k):
-        if self.ways[k] == "z":
-            for route, dx, dy in ((5, 0, 0), (8, 1, 0), (9, 0, 1), (10, 1, 1)):
-                self.arrive(self.block(k, dz=ALL4, dx=dx, dy=dy, dc=1), k, route)
-        else:
-            near, far = "d" + self.ways[k], "dy" if self.ways[k] == "x" else "dx"
-            for route in range(2):
-                self.arrive(self.block(k, **{near: ALL2, "dz": ALL4, far: route, "dc": 1}), k, 5 + route)
+        self.arrive(self.block(k, dy=ALL2, dz=ALL4, dx=ALL2), k, 4)
 
     def step(self, t):
         for late, move in enumerate((self.first, self.second, self.third, self.fourth, self.ready)):
@@ -459,8 +457,8 @@
                 move(t - late)
 
     def finish(self):
-        for copy in self.started:
-            copy.wait_send()
+        for k in range(len(self.parts) - DEPTH, len(self.parts)):
+            self.retire(k)
 
 
 F32, BF16 = jnp.float32, jnp.bfloat16
@@ -511,12 +509,12 @@
     def __init__(self, spot, out, into, send, recv):
         self.spot, self.out, self.into, self.send, self.recv = spot, out, into, send, recv
 
-    def copy(self, unit, step, source, target, peer):
+    def copy(self, unit, source, target, block, peer):
         return pltpu.make_async_remote_copy(
-            src_ref=self.out.at[unit, source],
-            dst_ref=self.into.at[unit, target],
-            send_sem=self.send.at[unit, step],
-            recv_sem=self.recv.at[unit, step],
+            src_ref=source,
+            dst_ref=target,
+            send_sem=self.send.at[unit, block],
+            recv_sem=self.recv.at[unit, self.spot.z],
             device_id=(self.spot.y, peer),
             device_id_type=MESH,
         )
@@ -529,7 +527,7 @@
 
             @pl.when(peer != me)
             def _():
-                self.copy(unit, (peer + 16 - me) % 16, peer, me, peer).start()
+                self.copy(unit, self.out.at[unit, peer], self.into.at[unit, me], block, peer).start()
 
             return carry
 
@@ -538,39 +536,23 @@
     def keep(self, unit):
         self.into[unit, self.spot.s] = self.out[unit, self.spot.s]
 
-    def wait_block(self, unit, block):
-        me = self.spot.s
-
-        def body(i, carry):
-            peer = block * 4 + i
-
-            @pl.when(peer != me)
-            def _():
-                self.copy(unit, (me + 16 - peer) % 16, peer, peer, peer).wait_recv()
-
-            return carry
-
-        lax.fori_loop(0, 4, body, 0)
+    def like(self, unit, far):
+        return self.into.at[unit, pl.ds(0, 4 if far else 3)]
+
+    def wait_block(self, unit, far):
+        block = (self.spot.z + far) % 4
+        like = self.like(unit, far)
+        pltpu.make_async_copy(like, like, self.recv.at[unit, block]).wait()
 
     def wait(self, unit):
-        me = self.spot.s
-
-        def body(step, carry):
-            peer = (me + 16 - step) % 16
-            self.copy(unit, step, peer, peer, peer).wait_recv()
-            return carry
-
-        lax.fori_loop(1, 16, body, 0)
+        for far in range(4):
+            self.wait_block(unit, far)
 
     def finish(self, units):
-        me = self.spot.s
-
-        def body(step, carry):
-            for unit in range(units):
-                self.copy(unit, step, (me + step) % 16, me, (me + step) % 16).wait_send()
-            return carry
-
-        lax.fori_loop(1, 16, body, 0)
+        for unit in range(units):
+            for far in range(4):
+                like = self.like(unit, far)
+                pltpu.make_async_copy(like, like, self.send.at[unit, (self.spot.z + far) % 4]).wait()
 
 
 class Scatter:
@@ -579,11 +561,9 @@
         self.own, self.core_in, self.core_sum = own, core_in, core_sum
         self.x_in, self.x_sum, self.into = x_in, x_sum, into
         self.send, self.recv = send, recv
-        self.started = []
-
-    def push(self, source, target, peer):
-        route = len(self.started)
-        copy = pltpu.make_async_remote_copy(
+
+    def copy(self, source, target, route, peer):
+        return pltpu.make_async_remote_copy(
             src_ref=source,
             dst_ref=target,
             send_sem=self.send.at[route],
@@ -591,52 +571,43 @@
             device_id=peer,
             device_id_type=MESH,
         )
-        copy.start()
-        self.started.append(copy)
 
     def first(self):
         p = self.spot
-        self.push(self.own.at[:, :, :, 1 - p.c], self.core_in, p.at(dc=1))
+        self.hop = self.copy(self.own.at[:, :, :, 1 - p.c], self.core_in, 0, p.at(dc=1))
+        self.hop.start()
 
     def second(self):
         p = self.spot
-        self.started[0].wait_recv()
+        self.hop.wait()
         self.core_sum[...] = (self.own[:, :, :, p.c].astype(F32) + self.core_in[...].astype(F32)).astype(BF16)
         if not self.wide:
-            self.push(self.core_sum.at[:, :, 1 - p.x], self.x_in, p.at(dx=1))
+            self.hop = self.copy(self.core_sum.at[:, :, 1 - p.x], self.x_in, 1, p.at(dx=1))
+            self.hop.start()
+
+    def distances(self):
+        every = [(dy, dz, dx) for dy in range(2) for dz in range(4) for dx in range(2 if self.wide else 1)]
+        return every[1:]
 
     def third(self):
         p = self.spot
         if not self.wide:
-            self.started[1].wait_recv()
+            self.hop.wait()
             self.x_sum[...] = (self.core_sum[:, :, p.x].astype(F32) + self.x_in[...].astype(F32)).astype(BF16)
-        for dy in range(2):
-            for dz in range(4):
-                for dx in range(2 if self.wide else 1):
-                    if dy + dz + dx == 0:
-                        continue
-                    y, z, x = (p.y + dy) % 2, (p.z + dz) % 4, (p.x + dx) % 2
-                    source = self.core_sum.at[y, z, x] if self.wide else self.x_sum.at[y, z]
-                    self.push(source, self.into.at[dy, dz, dx], p.at(dy=dy, dz=dz, dx=dx))
+        for n, (dy, dz, dx) in enumerate(self.distances()):
+            y, z, x = (p.y + dy) % 2, (p.z + dz) % 4, (p.x + dx) % 2
+            source = self.core_sum.at[y, z, x] if self.wide else self.x_sum.at[y, z]
+            self.copy(source, self.into.at[n], 2, p.at(dy=dy, dz=dz, dx=dx)).start()
 
     def fourth(self):
         p = self.spot
-        for copy in self.started[1 if self.wide else 2 :]:
-            copy.wait_recv()
+        self.copy(self.into, self.into, 2, p.at(dc=1)).wait()
         total = [self.core_sum[p.y, p.z, p.x] if self.wide else self.x_sum[p.y, p.z], None]
         total[0] = total[0].astype(F32)
-        for dy in range(2):
-            for dz in range(4):
-                for dx in range(2 if self.wide else 1):
-                    if dy + dz + dx == 0:
-                        continue
-                    term = self.into[dy, dz, dx].astype(F32)
-                    total[dy] = term if total[dy] is None else total[dy] + term
+        for n, (dy, _, _) in enumerate(self.distances()):
+            term = self.into[n].astype(F32)
+            total[dy] = term if total[dy] is None else total[dy] + term
         return total
-
-    def finish(self):
-        for copy in self.started:
-            copy.wait_send()
 
 
 def scatter_shapes(rows, wide):
@@ -646,9 +617,9 @@
         pltpu.VMEM((2, 4, 2, rows, 128), BF16),
         pltpu.VMEM((2, 4, rows, 128), BF16),
         pltpu.VMEM((2, 4, rows, 128), BF16),
-        pltpu.VMEM((2, 4, 2 if wide else 1, rows, 128), BF16),
-        pltpu.SemaphoreType.DMA((17,)),
-        pltpu.SemaphoreType.DMA((17,)),
+        pltpu.VMEM((15 if wide else 7, rows, 128), BF16),
+        pltpu.SemaphoreType.DMA((3,)),
+        pltpu.SemaphoreType.DMA((3,)),
     ]
 
 
@@ -674,18 +645,16 @@
     spot = Spot()
     here = (spot.y, spot.z, spot.x, spot.c)
     parts = [wide.at[k] for k in range(16)] + [tall.at[k] for k in range(8)] + [rank_all, ff_all]
-    placed = {}
-    for k in range(8, 16):
-        placed[k] = fc1.at[:, pl.ds((k - 8) * 512, 512)]
-    for k in range(16, 24):
-        placed[k] = fc2.at[:, pl.ds((k - 16) * 128, 128)]
-    placed = {k: pltpu.make_async_copy(source, parts[k].at[here], own.at[k - 8]) for k, source in placed.items()}
-    tok_copy = pltpu.make_async_copy(tok_far, tok, own.at[16])
-    cot_copy = pltpu.make_async_copy(cot_far, cot, own.at[17])
+    placed = []
+    for k in range(8):
+        placed.append(pltpu.make_async_copy(fc1.at[:, pl.ds(k * 512, 512)], parts[8 + k].at[here], own.at[0]))
+        placed.append(pltpu.make_async_copy(fc2.at[:, pl.ds(k * 128, 128)], parts[16 + k].at[here], own.at[1]))
+    tok_copy = pltpu.make_async_copy(tok_far, tok, own.at[2])
+    cot_copy = pltpu.make_async_copy(cot_far, cot, own.at[3])
     tok_copy.start()
     for k in (0, 1):
         wide[(k,) + here] = attn[:, 0, k * 512 : k * 512 + 512]
-    for copy in placed.values():
+    for copy in placed:
         copy.start()
     cot_copy.start()
     others = {2: rank_other, 3: ff_other}
@@ -982,7 +951,7 @@
 
     def query_back(t):
         block = (spot.z + 4 - t) % 4
-        swaps.wait_block(4, block)
+        swaps.wait_block(4, (4 - t) % 4)
         rows = tile(block)
         keys = heads_in[1].reshape(1024, 128)
         values = heads_in[2].reshape(1024, 128)
@@ -1085,19 +1054,13 @@
             for kind in range(2):
                 ff_out[a, kind] = gathered(ff_turned, kind * 32)
 
-    waited = set()
-
-    def here_by(last):
-        for k in ORDER[: last + 1]:
-            if k in placed and k not in waited:
-                placed[k].wait()
-                waited.add(k)
-
     for t in range(1, CHUNKS + 4):
         if t == 2:
             id_copy.wait_recv()
             pick_all()
-        here_by(min(t, CHUNKS - 1))
+        if t == 4:
+            for n, like in enumerate((wide.at[(pl.ds(8, 8),) + here], tall.at[(pl.ds(0, 8),) + here])):
+                pltpu.make_async_copy(like, like, own.at[n]).wait()
         gather.step(t)
         if t == 7:
             tok_copy.wait()
@@ -1142,8 +1105,6 @@
     id_copy.wait_send()
     gather.finish()
     swaps.finish(8)
-    early.finish()
-    late.finish()
 
 
 def hand_on_kernel(*refs):
@@ -1189,9 +1150,9 @@
     scratch += [buffer(2, 8, 128, dtype=jnp.int32), buffer(896, 128, dtype=F32)]
     scratch += [buffer(32, 384), buffer(80, 128)]
     scratch += scatter_shapes(EARLY, False) + scatter_shapes(LATE, True)
-    scratch += [pltpu.SemaphoreType.DMA((18,))]
-    scratch += [pltpu.SemaphoreType.DMA((CHUNKS, ROUTES))] * 2
-    scratch += [pltpu.SemaphoreType.DMA((8, 16))] * 2
+    scratch += [pltpu.SemaphoreType.DMA((4,))]
+    scratch += [pltpu.SemaphoreType.DMA((DEPTH, 4)), pltpu.SemaphoreType.DMA((DEPTH, 5))]
+    scratch += [pltpu.SemaphoreType.DMA((8, 4))] * 2
     scratch += [pltpu.SemaphoreType.DMA((2,))]
     return pl.pallas_call(
         layer_kernel,

time: 205 us -> 197 us (0.961)
  Pallas kernels: 205 us -> 196 us
    pallas_call x1, Pallas kernels: 202 us -> 194 us  [layer(): pl.pallas_call(layer_kernel, out_shape=[jax.ShapeDtypeStruct(tok.shape, B...]
where the time goes in v3:
time: 197 us
  Pallas kernels  196 us (99%)
    pallas_call x1, Pallas kernels, layer(): pl.pallas_call(layer_kernel, out_shape=[jax.ShapeDtypeStruct(tok.shape, B...  194 us

profile of v3, /device:TPU:0, one launch (start us, length us, event | category | flops | bytes accessed | tf_op | source)
XLA Modules:
  0.0 196.8 jit_solution(8089555059974925424)
XLA Ops:
  0.6 193.8 %layer.1 = (bf16[128,1024]{1,0:T(8,128)(2,1)}, bf16[128,1024]{1,0:T(8,128)(2,1)}, f32[8,5,16,32]{3,2,1,0:T(8,128)}, f32[8,5,16,32]{3,2,1,0:T(8,128)}, f32[8,2,16,128]{3,2,1,0:T(8,128)}) custom-call(bf16[32,4,1024]{2,1,0:T(4,128)(2,1)} %refs_0_.1, bf16[32,4096]{1,0:T(8,128)(2,1)} %refs_1_.1, bf16[128,1024]{1,0:T(8,128)(2,1)} %refs_2_.1, ...), custom_call_target="tpu_custom_call" | custom-call | tf_op jit(solution)/shard_map/layer/pallas_call | solution.py:1157
  194.5 2.3 %hand_on.1 = (bf16[128,1024]{1,0:T(8,128)(2,1)}, bf16[128,1024]{1,0:T(8,128)(2,1)}, f32[8,5,16,32]{3,2,1,0:T(8,128)}, f32[8,5,16,32]{3,2,1,0:T(8,128)}, f32[8,2,16,128]{3,2,1,0:T(8,128)}) custom-call(bf16[128,1024]{1,0:T(8,128)(2,1)} %get-tuple-element.15.refs_0_, bf16[128,1024]{1,0:T(8,128)(2,1)} %get-tuple-element.16.refs_1_, ...), custom_call_target="tpu_custom_call" | custom-call | tf_op jit(solution)/shard_map/hand_on/pallas_call | solution.py:1118

commit v4 on v3

--- a/solution.py
+++ b/solution.py
@@ -350,6 +350,8 @@
         self.z = self.s // 4
         self.x = (self.s // 2) % 2
         self.c = self.s % 2
+        self.pair_z = self.z + 1 - 2 * (self.z % 2)
+        self.inner = (self.z + 1) // 2 == 1
 
     def at(self, dy=0, dz=0, dx=0, dc=0):
         y = (self.y + dy) % 2
@@ -397,24 +399,63 @@
     def retire(self, k):
         if self.ways[k] == "z":
             pieces = ((1, 3, 1), (2, 3, 2), (2, 3, 2), (1, 4, 1))
+        elif self.ways[k] == "h":
+            pieces = ((1, 1, 1), (2, 3, 2), (2, 3, 2), (1, 4, 1))
+
+            @pl.when(self.spot.inner)
+            def _():
+                for out in (4, 5):
+                    like = self.pair_of(k, 0)
+                    self.copy(like, like, k, out, 0, self.spot.at(dc=1)).wait_send()
+
         else:
             pieces = ((1, 1, 1), (2, 3, 1), (2, 4, 2), (2, 4, 1))
         for out, (ys, zs, xs) in enumerate(pieces):
             like = self.parts[k].at[pl.ds(0, ys), pl.ds(0, zs), pl.ds(0, xs), 0]
             self.copy(like, like, k, out, 0, self.spot.at(dc=1)).wait_send()
 
+    def pair_of(self, k, far):
+        p = self.spot
+        return self.parts[k].at[p.y, pl.ds(((p.z // 2 + far) % 2) * 2, 2), p.x, p.c]
+
+    def hand(self, k):
+        self.arrive(self.block(k), k, 0)
+
+        @pl.when(self.spot.inner)
+        def _():
+            self.push_to(self.pair_of(k, 0), k, 4, 5, 3 - self.spot.z)
+
+    def pass_on(self, k):
+        @pl.when(self.spot.inner)
+        def _():
+            self.arrive(self.pair_of(k, 1), k, 5)
+            self.push_to(self.pair_of(k, 1), k, 5, 5, self.spot.pair_z)
+
+    def push_to(self, ref, k, out, into, z):
+        p = self.spot
+        self.copy(ref, ref, k, out, into, (p.y, (z * 2 + p.x) * 2 + p.c)).start()
+
     def first(self, k):
         if k >= DEPTH:
             self.retire(k - DEPTH)
-        if self.ways[k] == "z":
+        if self.ways[k] == "h":
+            self.push_to(self.block(k), k, 0, 0, self.spot.pair_z)
+        elif self.ways[k] == "z":
             for d in range(1, 4):
                 self.push(self.block(k), k, 0, 0, dz=d)
         else:
             self.push(self.block(k), k, 0, 0, self.others.get(k), **{"d" + self.ways[k]: 1})
 
     def second(self, k):
-        if self.ways[k] == "z":
-            self.arrive(self.block(k, dz=pl.ds(0, 3)), k, 0)
+        if self.ways[k] in "zh":
+            if self.ways[k] == "z":
+                self.arrive(self.block(k, dz=pl.ds(0, 3)), k, 0)
+            else:
+
+                @pl.when(jnp.logical_not(self.spot.inner))
+                def _():
+                    self.arrive(self.pair_of(k, 1), k, 5)
+
             line = self.block(k, dz=ALL4)
             self.push(line, k, 1, 1, dx=1)
             self.push(line, k, 1, 2, dy=1)
@@ -425,11 +466,12 @@
                 self.push(self.block(k, **{"d" + self.ways[k]: ALL2}), k, 1, 1, dz=d)
 
     def third(self, k):
-        if self.ways[k] == "z":
+        if self.ways[k] in "zh":
+            cut = 3 if k in SHIFTED else 2
             self.arrive(self.block(k, dz=ALL4), k, 1)
-            self.push(self.block(k, dz=pl.ds(0, 2), dx=1), k, 2, 3, dy=1)
+            self.push(self.block(k, dz=pl.ds(0, cut), dx=1), k, 2, 3, dy=1)
             self.arrive(self.block(k, dz=ALL4), k, 2)
-            self.push(self.block(k, dz=pl.ds(2, 2), dy=1), k, 2, 3, dx=1)
+            self.push(self.block(k, dz=pl.ds(cut, 4 - cut), dy=1), k, 2, 3, dx=1)
             self.push(self.block(k, dz=ALL4, dx=1), k, 2, 4, dc=1)
             self.push(self.block(k, dz=ALL4, dy=1), k, 2, 4, dc=1)
         else:
@@ -440,7 +482,7 @@
             self.push(plane, k, 2, 4, dc=1)
 
     def fourth(self, k):
-        if self.ways[k] == "z":
+        if self.ways[k] in "zh":
             self.arrive(self.block(k, dz=ALL4), k, 3)
             self.push(self.block(k, dz=ALL4, dx=1, dy=1), k, 3, 4, dc=1)
         else:
@@ -452,9 +494,12 @@
         self.arrive(self.block(k, dy=ALL2, dz=ALL4, dx=ALL2), k, 4)
 
     def step(self, t):
-        for late, move in enumerate((self.first, self.second, self.third, self.fourth, self.ready)):
-            if 0 <= t - late < len(self.parts):
-                move(t - late)
+        moves = ((0, self.first), (1, self.second), (2, self.third), (3, self.fourth), (4, self.ready))
+        hops = ((-2, self.first), (-1, self.hand), (0, self.pass_on)) + moves[1:]
+        order = [(late, k, move) for k, way in enumerate(self.ways) for late, move in (hops if way == "h" else moves)]
+        for late, k, move in sorted(order, key=lambda entry: (entry[0], entry[1])):
+            if k + late == t:
+                move(k)
 
     def finish(self):
         for k in range(len(self.parts) - DEPTH, len(self.parts)):
@@ -463,7 +508,8 @@
 
 F32, BF16 = jnp.float32, jnp.bfloat16
 ORDER = (0, 1, 24, 25) + tuple(range(2, 24))
-WAYS = "zzyyzzzzzzzzzzzzzzzzzzzzzz"
+WAYS = "zzyyzz" + "h" * 20
+SHIFTED = (6, 7, 8, 9, 10, 12, 13, 16)
 EARLY, LATE = 80, 64
 
 
@@ -997,23 +1043,19 @@
         swaps.keep(7)
 
     def inputs_back():
-        swaps.wait(5)
-        heads_to_rows(heads_in.at[5], query_low, 0.125)
-        swaps.wait(6)
-        heads_to_rows(heads_in.at[6], key_low, 1.0)
-        swaps.wait(7)
-        heads_to_rows(heads_in.at[7], value_low, 1.0)
         grads = (query_low, key_low, value_low)
         inner = jnp.zeros((128, 128), F32)
-        for j in range(3):
-            inner = jnp.where(kind4[j], dot(grads[j][...], rank_up[...]), inner)
+        ups = dot_tn(branch_low[...], saved["o"])
+        downs = dot_tn(mixed[...], saved["g_o"])
+        for j, grad in enumerate(grads):
+            swaps.wait(5 + j)
+            heads_to_rows(heads_in.at[5 + j], grad, 0.125 if j == 0 else 1.0)
+            inner = jnp.where(kind4[j], dot(grad[...], rank_up[...]), inner)
+            ups = ups + dot_tn(grad[...], only(kind4[j], inner4[...]))
         saved["g_in"] = inner.astype(BF16)
-        value = dot_tn(tok[...], saved["g_in"]) + dot_tn(mixed[...], saved["g_o"])
-        late.own[:, :, :, :, 0:32, :] = value.astype(BF16).reshape(2, 4, 2, 2, 32, 128)
-        value = dot_tn(branch_low[...], saved["o"])
-        for j in range(3):
-            value = value + dot_tn(grads[j][...], only(kind4[j], inner4[...]))
-        late.own[:, :, :, :, 32:64, :] = value.astype(BF16).reshape(2, 4, 2, 2, 32, 128)
+        late.own[:, :, :, :, 32:64, :] = ups.astype(BF16).reshape(2, 4, 2, 2, 32, 128)
+        downs = downs + dot_tn(tok[...], saved["g_in"])
+        late.own[:, :, :, :, 0:32, :] = downs.astype(BF16).reshape(2, 4, 2, 2, 32, 128)
 
     def tokens_back(t):
         rows = pl.ds(t * 256, 256)
@@ -1151,7 +1193,7 @@
     scratch += [buffer(32, 384), buffer(80, 128)]
     scratch += scatter_shapes(EARLY, False) + scatter_shapes(LATE, True)
     scratch += [pltpu.SemaphoreType.DMA((4,))]
-    scratch += [pltpu.SemaphoreType.DMA((DEPTH, 4)), pltpu.SemaphoreType.DMA((DEPTH, 5))]
+    scratch += [pltpu.SemaphoreType.DMA((DEPTH, 6))] * 2
     scratch += [pltpu.SemaphoreType.DMA((8, 4))] * 2
     scratch += [pltpu.SemaphoreType.DMA((2,))]
     return pl.pallas_call(

time: 197 us -> 188 us (0.954)
  Pallas kernels: 196 us -> 187 us
    pallas_call x1, Pallas kernels: 194 us -> 185 us  [layer(): pl.pallas_call(layer_kernel, out_shape=[jax.ShapeDtypeStruct(tok.shape, B...]
where the time goes in v4:
time: 188 us
  Pallas kernels  187 us (99%)
    pallas_call x1, Pallas kernels, layer(): pl.pallas_call(layer_kernel, out_shape=[jax.ShapeDtypeStruct(tok.shape, B...  185 us

profile of v4, /device:TPU:0, one launch (start us, length us, event | category | flops | bytes accessed | tf_op | source)
XLA Modules:
  0.0 188.0 jit_solution(2707109684108604435)
XLA Ops:
  0.6 185.0 %layer.1 = (bf16[128,1024]{1,0:T(8,128)(2,1)}, bf16[128,1024]{1,0:T(8,128)(2,1)}, f32[8,5,16,32]{3,2,1,0:T(8,128)}, f32[8,5,16,32]{3,2,1,0:T(8,128)}, f32[8,2,16,128]{3,2,1,0:T(8,128)}) custom-call(bf16[32,4,1024]{2,1,0:T(4,128)(2,1)} %refs_0_.1, bf16[32,4096]{1,0:T(8,128)(2,1)} %refs_1_.1, bf16[128,1024]{1,0:T(8,128)(2,1)} %refs_2_.1, ...), custom_call_target="tpu_custom_call" | custom-call | tf_op jit(solution)/shard_map/layer/pallas_call | solution.py:1199
  185.7 2.3 %hand_on.1 = (bf16[128,1024]{1,0:T(8,128)(2,1)}, bf16[128,1024]{1,0:T(8,128)(2,1)}, f32[8,5,16,32]{3,2,1,0:T(8,128)}, f32[8,5,16,32]{3,2,1,0:T(8,128)}, f32[8,2,16,128]{3,2,1,0:T(8,128)}) custom-call(bf16[128,1024]{1,0:T(8,128)(2,1)} %get-tuple-element.15.refs_0_, bf16[128,1024]{1,0:T(8,128)(2,1)} %get-tuple-element.16.refs_1_, ...), custom_call_target="tpu_custom_call" | custom-call | tf_op jit(solution)/shard_map/hand_on/pallas_call | solution.py:1160

commit v5 on v4

--- a/solution.py
+++ b/solution.py
@@ -510,7 +510,8 @@
 ORDER = (0, 1, 24, 25) + tuple(range(2, 24))
 WAYS = "zzyyzz" + "h" * 20
 SHIFTED = (6, 7, 8, 9, 10, 12, 13, 16)
-EARLY, LATE = 80, 64
+EARLY, LATE = 80, 32
+FAR_FIRST = (2, 1, 3, 0)
 
 
 def dot(left, right):
@@ -676,7 +677,7 @@
         return [next(it) for _ in range(count)]
 
     attn, fc1, fc2, tok_far, cot_far, down_table, up_table, ff_table, vec_in, bias_in, lengths, ids = take(12)
-    layer_out, input_grad, down_out, up_out, ff_out = take(5)
+    layer_out, input_grad, sums_out, ids_out = take(4)
     wide, tall, rank_all, ff_all = take(4)
     rank_in, rank_up, rank_x, vec, ff_low, bias = take(6)
     heads_out, heads_in = take(2)
@@ -685,16 +686,15 @@
     tok, cot, mixed, normed_low, out_low, branch_low, query_low, key_low, value_low = take(9)
     slope, act, grad_hidden, inner4 = take(4)
     id_rows, table, rank_other, ff_other = take(4)
-    early_refs, late_refs = take(8), take(8)
+    early_refs, up_refs, down_refs = take(8), take(8), take(8)
     own, send, recv, hsend, hrecv, id_sem = take(6)
 
     spot = Spot()
     here = (spot.y, spot.z, spot.x, spot.c)
     parts = [wide.at[k] for k in range(16)] + [tall.at[k] for k in range(8)] + [rank_all, ff_all]
-    placed = []
+    placed = [pltpu.make_async_copy(fc2, query_low, own.at[1])]
     for k in range(8):
         placed.append(pltpu.make_async_copy(fc1.at[:, pl.ds(k * 512, 512)], parts[8 + k].at[here], own.at[0]))
-        placed.append(pltpu.make_async_copy(fc2.at[:, pl.ds(k * 128, 128)], parts[16 + k].at[here], own.at[1]))
     tok_copy = pltpu.make_async_copy(tok_far, tok, own.at[2])
     cot_copy = pltpu.make_async_copy(cot_far, cot, own.at[3])
     tok_copy.start()
@@ -707,7 +707,8 @@
     gather = Gather(spot, [parts[k] for k in ORDER], WAYS, others, send, recv)
     swaps = Exchange(spot, heads_out, heads_in, hsend, hrecv)
     early = Scatter(spot, False, *early_refs)
-    late = Scatter(spot, True, *late_refs)
+    late_up = Scatter(spot, True, *up_refs)
+    late_down = Scatter(spot, True, *down_refs)
     first_row = lax.broadcasted_iota(jnp.int32, (8, 128), 0) == 0
     id_rows[spot.y] = jnp.where(first_row, ids[0], ids[1])
     enter(spot)
@@ -810,12 +811,16 @@
             heads_out[unit, block * 4 + 2 * p + 1] = pair(swap(first), second).astype(BF16)
         swaps.start(unit, block)
 
-    def turn(body):
+    def turn(body, unrolled=False):
         def shifted(t, carry):
             body((spot.z + t) % 4)
             return carry
 
-        lax.fori_loop(0, 4, shifted, 0)
+        if unrolled:
+            for t in FAR_FIRST:
+                shifted(t, 0)
+        else:
+            lax.fori_loop(0, 4, shifted, 0)
 
     def project_in(j):
         inner = only(kind4[j], inner4[...])
@@ -927,8 +932,11 @@
         if q == 0:
             saved["out"] = only(kind_ff[1], dot(act[...], ff_rows(0, 32))).astype(BF16)
         cols = slice(q * 256, q * 256 + 256)
-        weight = jnp.concatenate([tall[2 * q + i].reshape(4096, 128) for i in range(2)], axis=1)
-        value = dot(act[...], weight) + dot_nt(saved["out"], rank_x[cols, :])
+        halves = []
+        for k in (2 * q, 2 * q + 1):
+            places = [(o // 16, (o // 4) % 4, (o // 2) % 2, o % 2) for o in range(32)]
+            halves.append(jnp.concatenate([tall[(k,) + place] for place in places], axis=1))
+        value = dot_nt(act[...], jnp.concatenate(halves, axis=0)) + dot_nt(saved["out"], rank_x[cols, :])
         tmp[:, cols] = normed[:, cols] + value + vec[3:4, cols]
 
     def outer():
@@ -945,16 +953,14 @@
 
     def hidden_back():
         def body(t, carry):
-            rows = tile(t, 512)
-            value = dot_nt(saved["g_out"], ff_rows(t * 4, 4))
-            for q in range(4):
-                pieces = [tall[2 * q + i, t // 4, t % 4].reshape(512, 128) for i in range(2)]
-                piece = jnp.concatenate(pieces, axis=1)
-                value = value + dot_nt(out_low[:, q * 256 : q * 256 + 256], piece)
+            rows = tile(t)
+            pieces = [tall[:, t // 8, (t // 2) % 4, t % 2, c].reshape(1024, 128) for c in range(2)]
+            value = dot(out_low[...], jnp.concatenate(pieces, axis=1))
+            value = value + dot_nt(saved["g_out"], ff_rows(t * 2, 2))
             grad_hidden[:, rows] = (value * slope[:, rows]).astype(BF16)
             return carry
 
-        lax.fori_loop(0, 8, body, 0)
+        lax.fori_loop(0, 16, body, 0, unroll=True)
         saved["g_hidden"] = only(kind_ff[0], dot(grad_hidden[...], ff_rows(0, 32))).astype(BF16)
 
     def normed_back():
@@ -966,7 +972,7 @@
             tmp[:, rows] = value
             return carry
 
-        lax.fori_loop(0, 4, body, 0)
+        lax.fori_loop(0, 4, body, 0, unroll=True)
         grad = normalize_back(tmp[...] * vec[4:5], scaled_one[...], saved["spread_one"])
         grad_first[...] = grad
         branch_low[...] = grad.astype(BF16)
@@ -977,7 +983,7 @@
             value = dot_nt(branch_low[...], square(3, n)) + dot_nt(saved["g_o"], rank_in[tile(n), :])
             to_heads(4, n, value)
 
-        turn(body)
+        turn(body, True)
         swaps.keep(4)
 
     def early_grads():
@@ -1014,7 +1020,7 @@
         heads_out[5, pl.ds(block * 4, 4)] = pair(*parts_).astype(BF16).reshape(4, 64, 128)
         stat[rows, :] = pair(*deltas)
         swaps.start(5, block)
-        if t == 3:
+        if t == FAR_FIRST[-1]:
             swaps.keep(5)
 
     def key_back():
@@ -1038,24 +1044,31 @@
             swaps.start(6, block)
             swaps.start(7, block)
 
-        turn(body)
+        turn(body, True)
         swaps.keep(6)
         swaps.keep(7)
 
     def inputs_back():
         grads = (query_low, key_low, value_low)
-        inner = jnp.zeros((128, 128), F32)
         ups = dot_tn(branch_low[...], saved["o"])
         downs = dot_tn(mixed[...], saved["g_o"])
         for j, grad in enumerate(grads):
             swaps.wait(5 + j)
             heads_to_rows(heads_in.at[5 + j], grad, 0.125 if j == 0 else 1.0)
+            ups = ups + dot_tn(grad[...], only(kind4[j], inner4[...]))
+        late_up.own[...] = ups.astype(BF16).reshape(2, 4, 2, 2, 32, 128)
+        late_up.first()
+        inner = jnp.zeros((128, 128), F32)
+        for j, grad in enumerate(grads):
             inner = jnp.where(kind4[j], dot(grad[...], rank_up[...]), inner)
-            ups = ups + dot_tn(grad[...], only(kind4[j], inner4[...]))
         saved["g_in"] = inner.astype(BF16)
-        late.own[:, :, :, :, 32:64, :] = ups.astype(BF16).reshape(2, 4, 2, 2, 32, 128)
         downs = downs + dot_tn(tok[...], saved["g_in"])
-        late.own[:, :, :, :, 0:32, :] = downs.astype(BF16).reshape(2, 4, 2, 2, 32, 128)
+        late_down.own[...] = downs.astype(BF16).reshape(2, 4, 2, 2, 32, 128)
+        late_down.first()
+        late_up.second()
+        late_up.third()
+        late_down.second()
+        late_down.third()
 
     def tokens_back(t):
         rows = pl.ds(t * 256, 256)
@@ -1064,45 +1077,17 @@
             value = value + dot_nt(grad[...], square(j, t))
         input_grad[:, rows] = value.astype(BF16)
 
-    def results(early_sum, late_sum):
-        turned, ff_turned = [], []
-        for dy in range(2):
-            cross = jnp.concatenate([early_sum[dy][0:16], swap(early_sum[dy][0:16])], axis=0)
-            table[0:64, :] = late_sum[dy]
-            table[64:96, :] = cross
-            table[96:128, :] = jnp.zeros((32, 128), F32)
-            turned.append(table[0:128, :].T)
-            packed = early_sum[dy][16:80]
-            ff_turned.append(jnp.concatenate([packed, swap(packed)], axis=0).T)
-        for a in range(ADAPTERS):
-            who = [id_rows[(spot.y + dy) % 2, 0:2, :] == a for dy in range(2)]
-            share = [match.astype(F32) for match in who]
-
-            def gathered(source, first):
-                total = None
-                for dy in range(2):
-                    for s in range(2):
-                        row = first + s * 16
-                        term = share[dy][s : s + 1] * source[dy][row : row + 16, :]
-                        total = term if total is None else total + term
-                return total
-
-            for j in range(4):
-                value = gathered(turned, j * 32)
-                down_out[a, j] = value[:, 0:32]
-                up_out[a, j] = value[:, 32:64]
-            down_out[a, 4] = gathered(turned, 0)[:, 64:96]
-            up_out[a, 4] = gathered(turned, 32)[:, 64:96]
-            for kind in range(2):
-                ff_out[a, kind] = gathered(ff_turned, kind * 32)
-
     for t in range(1, CHUNKS + 4):
         if t == 2:
             id_copy.wait_recv()
             pick_all()
         if t == 4:
-            for n, like in enumerate((wide.at[(pl.ds(8, 8),) + here], tall.at[(pl.ds(0, 8),) + here])):
-                pltpu.make_async_copy(like, like, own.at[n]).wait()
+            like = wide.at[(pl.ds(8, 8),) + here]
+            pltpu.make_async_copy(like, like, own.at[0]).wait()
+            placed[0].wait()
+            for k in range(8):
+                turned = query_low[:, k * 128 : k * 128 + 128].astype(F32).T
+                tall[(k,) + here] = turned.astype(BF16)
         gather.step(t)
         if t == 7:
             tok_copy.wait()
@@ -1131,37 +1116,64 @@
     mixed_back()
     early_grads()
     early.first()
-    for t in range(4):
+    for t in FAR_FIRST:
         query_back(t)
     early.second()
     key_back()
     early.third()
     inputs_back()
-    late.first()
-    tokens_back(0)
-    late.second()
-    late.third()
-    for t in range(1, 4):
+    for t in range(4):
         tokens_back(t)
-    results(early.fourth(), late.fourth())
+    for first, scatter in ((0, early), (EARLY, late_down), (EARLY + LATE, late_up)):
+        for dy, total in enumerate(scatter.fourth()):
+            sums_out[dy, first : first + total.shape[0], :] = total
+    for dy in range(2):
+        ids_out[dy] = id_rows[(spot.y + dy) % 2]
     id_copy.wait_send()
     gather.finish()
     swaps.finish(8)
 
 
-def hand_on_kernel(*refs):
-    count = len(refs) // 2
-    for k in range(count):
-        refs[count + k][...] = refs[k][...]
-
-
-def hand_on(arrays):
+def hand_on_kernel(layer_in, grad_in, sums, ids, layer_out, grad_out, down_out, up_out, ff_out):
+    layer_out[...] = layer_in[...]
+    grad_out[...] = grad_in[...]
+    turned, ff_turned = [], []
+    for dy in range(2):
+        packed = sums[dy, 16:80, :]
+        ff_turned.append(jnp.concatenate([packed, swap(packed)], axis=0).T)
+        cross = sums[dy, 0:16, :]
+        rows = [sums[dy, EARLY : EARLY + 2 * LATE, :], cross, swap(cross), jnp.zeros((32, 128), F32)]
+        turned.append(jnp.concatenate(rows, axis=0).T)
+    for a in range(ADAPTERS):
+        share = [(ids[dy, 0:2, :] == a).astype(F32) for dy in range(2)]
+
+        def spread(source, first):
+            total = None
+            for dy in range(2):
+                for slot in range(2):
+                    row = first + slot * 16
+                    term = share[dy][slot : slot + 1] * source[dy][row : row + 16, :]
+                    total = term if total is None else total + term
+            return total
+
+        for j in range(4):
+            value = spread(turned, j * 32)
+            down_out[a, j] = value[:, 0:32]
+            up_out[a, j] = value[:, 32:64]
+        down_out[a, 4] = spread(turned, 0)[:, 64:96]
+        up_out[a, 4] = spread(turned, 32)[:, 64:96]
+        for kind in range(2):
+            ff_out[a, kind] = spread(ff_turned, kind * 32)
+
+
+def hand_on(arrays, shapes):
     near = pl.BlockSpec(memory_space=pltpu.VMEM)
     return pl.pallas_call(
         hand_on_kernel,
-        out_shape=[jax.ShapeDtypeStruct(array.shape, array.dtype) for array in arrays],
-        in_specs=[near] * len(arrays),
-        out_specs=[near] * len(arrays),
+        out_shape=[jax.ShapeDtypeStruct(array.shape, array.dtype) for array in arrays[:2]]
+        + [jax.ShapeDtypeStruct(shape, F32) for shape in shapes],
+        in_specs=[near] * 4,
+        out_specs=[near] * 5,
         name="hand_on",
     )(*arrays)
 
@@ -1191,7 +1203,7 @@
     scratch += [buffer(128, 4096, dtype=F32), buffer(128, 4096), buffer(128, 4096), buffer(128, 128)]
     scratch += [buffer(2, 8, 128, dtype=jnp.int32), buffer(896, 128, dtype=F32)]
     scratch += [buffer(32, 384), buffer(80, 128)]
-    scratch += scatter_shapes(EARLY, False) + scatter_shapes(LATE, True)
+    scratch += scatter_shapes(EARLY, False) + scatter_shapes(LATE, True) * 2
     scratch += [pltpu.SemaphoreType.DMA((4,))]
     scratch += [pltpu.SemaphoreType.DMA((DEPTH, 6))] * 2
     scratch += [pltpu.SemaphoreType.DMA((8, 4))] * 2
@@ -1201,12 +1213,11 @@
         out_shape=[
             jax.ShapeDtypeStruct(tok.shape, BF16),
             jax.ShapeDtypeStruct(tok.shape, BF16),
-            jax.ShapeDtypeStruct(down.shape, F32),
-            jax.ShapeDtypeStruct(up.shape, F32),
-            jax.ShapeDtypeStruct(ff.shape, F32),
+            jax.ShapeDtypeStruct((2, EARLY + 2 * LATE, 128), F32),
+            jax.ShapeDtypeStruct((2, 8, 128), jnp.int32),
         ],
         in_specs=[near] + [anywhere] * 4 + [near] * 5 + [scalar] * 2,
-        out_specs=[near] * 5,
+        out_specs=[near] * 4,
         scratch_shapes=scratch,
         compiler_params=pltpu.CompilerParams(
             collective_id=0, has_side_effects=True, vmem_limit_bytes=63 * 2**20
@@ -1230,21 +1241,20 @@
     ff_adapters,
 ):
     width = tokens.shape[2]
+    tables = [table.transpose(1, 2, 3, 0) for table in (adapter_down, adapter_up, ff_adapters)]
     outs = layer(
         attn_weight,
         fc1_weight,
         fc2_weight,
         tokens.reshape(-1, width),
         cotangent.reshape(-1, width),
-        adapter_down.transpose(1, 2, 3, 0),
-        adapter_up.transpose(1, 2, 3, 0),
-        ff_adapters.transpose(1, 2, 3, 0),
+        *tables,
         vectors.T,
         fc1_bias[None],
         lengths,
         adapter_ids,
     )
-    outs = hand_on(outs)
+    outs = hand_on(outs, [table.shape for table in tables])
     grads = [grad.transpose(3, 0, 1, 2) for grad in outs[2:]]
     return (outs[0].reshape(tokens.shape), outs[1].reshape(tokens.shape), *grads)
 

time: 188 us -> 185 us (0.984)
  Pallas kernels: 187 us -> 184 us
    pallas_call x1, Pallas kernels: 185 us -> 181 us  [layer(): pl.pallas_call(layer_kernel, out_shape=[jax.ShapeDtypeStruct(tok.shape, B...]
where the time goes in v5:
time: 185 us; the launch traced here: 184 us
  Pallas kernels  184 us (99%)
    pallas_call x1, Pallas kernels, layer(): pl.pallas_call(layer_kernel, out_shape=[jax.ShapeDtypeStruct(tok.shape, B...  181 us

profile of v5, /device:TPU:0, one launch (start us, length us, event | category | flops | bytes accessed | tf_op | source)
XLA Modules:
  0.0 184.4 jit_solution(4213639110803054236)
XLA Ops:
  0.6 181.3 %layer.1 = (bf16[128,1024]{1,0:T(8,128)(2,1)}, bf16[128,1024]{1,0:T(8,128)(2,1)}, f32[2,144,128]{2,1,0:T(8,128)}, s32[2,8,128]{2,1,0:T(8,128)}) custom-call(bf16[32,4,1024]{2,1,0:T(4,128)(2,1)} %refs_0_.1, bf16[32,4096]{1,0:T(8,128)(2,1)} %refs_1_.1, bf16[128,1024]{1,0:T(8,128)(2,1)} %refs_2_.1, bf16[128,1024]{1,0:T(8,128)(2,1)} %bitcast.12, ...), custom_call_target="tpu_custom_call" | custom-call | tf_op jit(solution)/shard_map/layer/pallas_call | solution.py:1211
  182.0 2.4 %hand_on.1 = (bf16[128,1024]{1,0:T(8,128)(2,1)}, bf16[128,1024]{1,0:T(8,128)(2,1)}, f32[8,5,16,32]{3,2,1,0:T(8,128)}, f32[8,5,16,32]{3,2,1,0:T(8,128)}, f32[8,2,16,128]{3,2,1,0:T(8,128)}) custom-call(bf16[128,1024]{1,0:T(8,128)(2,1)} %get-tuple-element.14.layer_in, bf16[128,1024]{1,0:T(8,128)(2,1)} %get-tuple-element.15.grad_in, ...), custom_call_target="tpu_custom_call" | custom-call | tf_op jit(solution)/shard_map/hand_on/pallas_call | solution.py:1171

commit v6 on v5

--- a/solution.py
+++ b/solution.py
@@ -340,6 +340,7 @@
 MESH = pl.DeviceIdType.MESH
 CHUNKS = 26
 DEPTH = 8
+BY_BLOCK = 4
 ALL2, ALL4 = pl.ds(0, 2), pl.ds(0, 4)
 
 
@@ -556,12 +557,15 @@
     def __init__(self, spot, out, into, send, recv):
         self.spot, self.out, self.into, self.send, self.recv = spot, out, into, send, recv
 
-    def copy(self, unit, source, target, block, peer):
+    def arrived(self, unit, z):
+        return self.recv.at[unit if unit != BY_BLOCK else 8 + z]
+
+    def copy(self, unit, source, target, peer):
         return pltpu.make_async_remote_copy(
             src_ref=source,
             dst_ref=target,
-            send_sem=self.send.at[unit, block],
-            recv_sem=self.recv.at[unit, self.spot.z],
+            send_sem=self.send.at[unit],
+            recv_sem=self.arrived(unit, self.spot.z),
             device_id=(self.spot.y, peer),
             device_id_type=MESH,
         )
@@ -574,7 +578,7 @@
 
             @pl.when(peer != me)
             def _():
-                self.copy(unit, self.out.at[unit, peer], self.into.at[unit, me], block, peer).start()
+                self.copy(unit, self.out.at[unit, peer], self.into.at[unit, me], peer).start()
 
             return carry
 
@@ -583,23 +587,18 @@
     def keep(self, unit):
         self.into[unit, self.spot.s] = self.out[unit, self.spot.s]
 
-    def like(self, unit, far):
-        return self.into.at[unit, pl.ds(0, 4 if far else 3)]
-
-    def wait_block(self, unit, far):
-        block = (self.spot.z + far) % 4
-        like = self.like(unit, far)
-        pltpu.make_async_copy(like, like, self.recv.at[unit, block]).wait()
+    def wait_block(self, far):
+        like = self.into.at[BY_BLOCK, pl.ds(0, 4 if far else 3)]
+        pltpu.make_async_copy(like, like, self.arrived(BY_BLOCK, (self.spot.z + far) % 4)).wait()
 
     def wait(self, unit):
-        for far in range(4):
-            self.wait_block(unit, far)
+        like = self.into.at[unit, pl.ds(0, 15)]
+        pltpu.make_async_copy(like, like, self.recv.at[unit]).wait()
 
     def finish(self, units):
         for unit in range(units):
-            for far in range(4):
-                like = self.like(unit, far)
-                pltpu.make_async_copy(like, like, self.send.at[unit, (self.spot.z + far) % 4]).wait()
+            like = self.out.at[unit, pl.ds(0, 15)]
+            pltpu.make_async_copy(like, like, self.send.at[unit]).wait()
 
 
 class Scatter:
@@ -1003,7 +1002,7 @@
 
     def query_back(t):
         block = (spot.z + 4 - t) % 4
-        swaps.wait_block(4, (4 - t) % 4)
+        swaps.wait_block((4 - t) % 4)
         rows = tile(block)
         keys = heads_in[1].reshape(1024, 128)
         values = heads_in[2].reshape(1024, 128)
@@ -1206,7 +1205,7 @@
     scratch += scatter_shapes(EARLY, False) + scatter_shapes(LATE, True) * 2
     scratch += [pltpu.SemaphoreType.DMA((4,))]
     scratch += [pltpu.SemaphoreType.DMA((DEPTH, 6))] * 2
-    scratch += [pltpu.SemaphoreType.DMA((8, 4))] * 2
+    scratch += [pltpu.SemaphoreType.DMA((8,)), pltpu.SemaphoreType.DMA((12,))]
     scratch += [pltpu.SemaphoreType.DMA((2,))]
     return pl.pallas_call(
         layer_kernel,

time: 185 us -> 184 us (level)
  no operation moved by 1% of the time
where the time goes in v6:
time: 184 us
  Pallas kernels  183 us (99%)
    pallas_call x1, Pallas kernels, layer(): pl.pallas_call(layer_kernel, out_shape=[jax.ShapeDtypeStruct(tok.shape, B...  181 us

profile of v6, /device:TPU:0, one launch (start us, length us, event | category | flops | bytes accessed | tf_op | source)
XLA Modules:
  0.0 184.1 jit_solution(6987215970154202079)
XLA Ops:
  0.6 181.0 %layer.1 = (bf16[128,1024]{1,0:T(8,128)(2,1)}, bf16[128,1024]{1,0:T(8,128)(2,1)}, f32[2,144,128]{2,1,0:T(8,128)}, s32[2,8,128]{2,1,0:T(8,128)}) custom-call(bf16[32,4,1024]{2,1,0:T(4,128)(2,1)} %refs_0_.1, bf16[32,4096]{1,0:T(8,128)(2,1)} %refs_1_.1, bf16[128,1024]{1,0:T(8,128)(2,1)} %refs_2_.1, bf16[128,1024]{1,0:T(8,128)(2,1)} %bitcast.12, ...), custom_call_target="tpu_custom_call" | custom-call | tf_op jit(solution)/shard_map/layer/pallas_call | solution.py:1210
  181.6 2.4 %hand_on.1 = (bf16[128,1024]{1,0:T(8,128)(2,1)}, bf16[128,1024]{1,0:T(8,128)(2,1)}, f32[8,5,16,32]{3,2,1,0:T(8,128)}, f32[8,5,16,32]{3,2,1,0:T(8,128)}, f32[8,2,16,128]{3,2,1,0:T(8,128)}) custom-call(bf16[128,1024]{1,0:T(8,128)(2,1)} %get-tuple-element.14.layer_in, bf16[128,1024]{1,0:T(8,128)(2,1)} %get-tuple-element.15.grad_in, ...), custom_call_target="tpu_custom_call" | custom-call | tf_op jit(solution)/shard_map/hand_on/pallas_call | solution.py:1170
